TPU v7x, 128 devices: a whole 4x4x4 slice. The times are simulated.
128 devices in a mesh: seq: 8 (over z, core), ctx: 8 (over x, y_hi), tp: 2 (over y_lo).
Axes of the slice: x: 4, y: 4 (y_hi: 2, y_lo: 2; y = y_hi * 2 + y_lo), z: 4, core: 2. Of those that a mesh axis runs over, the one named last changes fastest.
Arguments:
- tokens: bfloat16 [8, 2048, 1024], P('seq', 'ctx'), may hold values from -6 to 6
- positions: int32 [8, 2048], P('seq', 'ctx'), may hold values from 0 to 2047, as said below
- cotangent: bfloat16 [8, 2048, 1024], P('seq', 'ctx'), may hold values from -6 to 6
- ln_gain: float32 [1024], replicated, may hold values from 0.5 to 1.5
- ln_bias: float32 [1024], replicated, may hold values from -3 to 3
- qkv_weight: bfloat16 [1024, 3, 1024], P(None, None, 'tp'), may hold values from -0.1875 to 0.1875
- out_weight: bfloat16 [1024, 1024], P('tp'), may hold values from -2 to 2
- fc_in_weight: bfloat16 [1024, 4096], P(None, 'tp'), may hold values from -0.1875 to 0.1875
- fc_in_bias: float32 [4096], P('tp'), may hold values from -3 to 3
- fc_out_weight: bfloat16 [4096, 1024], P('tp'), may hold values from -0.09375 to 0.09375
- fc_out_bias: float32 [1024], replicated, may hold values from -3 to 3
Outputs:
- block_out: bfloat16 [8, 2048, 1024], P('seq', 'ctx')
- tokens_grad: float32 [8, 2048, 1024], P('seq', 'ctx')
- ln_gain_grad: float32 [1024], replicated
- ln_bias_grad: float32 [1024], replicated
- qkv_grad: float32 [1024, 3, 1024], P(None, None, 'tp')
- out_grad: float32 [1024, 1024], P('tp')
- fc_in_grad: float32 [1024, 4096], P(None, 'tp')
- fc_in_bias_grad: float32 [4096], P('tp')
- fc_out_grad: float32 [4096, 1024], P('tp')
- fc_out_bias_grad: float32 [1024], replicated
Inputs may be any that keep to these rules, and one draw needn't show every extreme that they name: Each sequence's positions take every value of 0 to 2047 once; the 256 positions on one device are consecutive and rising, starting at a multiple of 256.
All inputs are finite; a program needn't handle non-finite values.
Results may differ from a plain program's by a relative error of at most 0.023.
Values may be sent and summed in bfloat16 or wider, within the bound.
A program may use at most 256 MiB of HBM per device.

v0:
```python
import math

import jax
import jax.numpy as jnp
from jax import lax
from jax.sharding import PartitionSpec as P

HD = 64
ROT = 32


eps_norm = 1e-05


def angle_tables(places):
    frequency = jnp.exp(jnp.arange(ROT // 2, dtype=jnp.float32) * (-2.0 * math.log(10000.0) / ROT))
    turned = places.astype(jnp.float32)[:, None] * frequency[None, :]
    return (jnp.cos(turned)[:, None, :], jnp.sin(turned)[:, None, :])


def rotate(vectors, cosine, sine_table):
    lead_shape = vectors.shape[:-1]
    paired = vectors[..., :ROT].reshape(lead_shape + (ROT // 2, 2))
    first_part = paired[..., 0]
    second_part = paired[..., 1]
    turned = jnp.stack(
        [
            first_part * cosine - second_part * sine_table,
            second_part * cosine + first_part * sine_table,
        ],
        axis=-1,
    )
    return jnp.concatenate([turned.reshape(lead_shape + (ROT,)), vectors[..., ROT:]], axis=-1)


def unrotate(vectors, cosine, sine_table):
    return rotate(vectors, cosine, -sine_table)


def normalize(inputs, ln_gain, ln_bias):
    mean_value = jnp.mean(inputs, axis=-1, keepdims=True)
    centered = inputs - mean_value
    variance = jnp.mean(centered * centered, axis=-1, keepdims=True)
    inv_std = lax.rsqrt(variance + eps_norm)
    x_hat = centered * inv_std
    return (x_hat, inv_std, (x_hat * ln_gain + ln_bias).astype(jnp.bfloat16))


def project(normed, qkv_weight, cosine, sine_table):
    model_width, _, local_width = qkv_weight.shape
    row_count = normed.shape[0]
    head_count = local_width // HD
    projected = jnp.dot(
        normed, qkv_weight.reshape(model_width, 3 * local_width), preferred_element_type=jnp.float32
    )
    queries = rotate(
        projected[:, :local_width].reshape(row_count, head_count, HD), cosine, sine_table
    ).astype(jnp.bfloat16)
    key_rot = rotate(
        projected[:, local_width : 2 * local_width].reshape(row_count, head_count, HD),
        cosine,
        sine_table,
    ).astype(jnp.bfloat16)
    value_rows = projected[:, 2 * local_width :].astype(jnp.bfloat16)
    return (queries, key_rot.reshape(row_count, local_width), value_rows)


def masked_scores(queries, key_all, own_places, key_places):
    head_count = queries.shape[1]
    key_three = key_all.reshape(key_all.shape[0], head_count, HD)
    scores = jnp.einsum(
        "qhd,khd->hqk", queries, key_three, preferred_element_type=jnp.float32
    ) * HD ** (-0.5)
    allowed = key_places[None, :] <= own_places[:, None]
    return jnp.where(allowed[None], scores, -1e30)


def softmax_parts(scores):
    row_max = jnp.max(scores, axis=-1, keepdims=True)
    row_total = jnp.sum(jnp.exp(scores - row_max), axis=-1, keepdims=True)
    return (row_max, row_total)


def weigh_values(prob_low, value_all, head_count):
    value_three = value_all.reshape(value_all.shape[0], head_count, HD)
    return jnp.einsum("hqk,khd->qhd", prob_low, value_three, preferred_element_type=jnp.float32)


def gelu_tanh(hidden):
    return jax.nn.gelu(hidden, approximate=True)


def norm_back(grad_in, x_hat, inv_std, ln_gain):
    scaled = grad_in * ln_gain
    mean_first = jnp.mean(scaled, axis=-1, keepdims=True)
    mean_second = jnp.mean(scaled * x_hat, axis=-1, keepdims=True)
    grad_rows = inv_std * (scaled - mean_first - x_hat * mean_second)
    return (grad_rows, jnp.sum(grad_in * x_hat, axis=0), jnp.sum(grad_in, axis=0))


def local(
    tokens,
    positions,
    cotangent,
    ln_gain,
    ln_bias,
    qkv_weight,
    out_weight,
    fc_in_weight,
    fc_in_bias,
    fc_out_weight,
    fc_out_bias,
):
    inputs = tokens[0].astype(jnp.float32)
    row_count, model_width = inputs.shape
    local_width = qkv_weight.shape[2]
    head_count = local_width // HD
    score_scale = HD ** (-0.5)
    own_places = positions[0]
    key_places = lax.all_gather(positions, "ctx", axis=1, tiled=True)[0]
    cosine, sine_table = angle_tables(own_places)
    x_hat, inv_std, normed = normalize(inputs, ln_gain, ln_bias)
    queries, key_rows, value_rows = project(normed, qkv_weight, cosine, sine_table)
    key_all, value_all = (
        lax.all_gather(key_rows, "ctx", axis=0, tiled=True),
        lax.all_gather(value_rows, "ctx", axis=0, tiled=True),
    )
    scores = masked_scores(queries, key_all, own_places, key_places)
    row_max, row_total = softmax_parts(scores)
    prob_low = (jnp.exp(scores - row_max) / row_total).astype(jnp.bfloat16)
    attended = weigh_values(prob_low, value_all, head_count)
    attended_low = attended.reshape(row_count, local_width).astype(jnp.bfloat16)
    hidden_pre = jnp.dot(normed, fc_in_weight, preferred_element_type=jnp.float32) + fc_in_bias
    activated = gelu_tanh(hidden_pre).astype(jnp.bfloat16)
    partial_sum = jnp.dot(attended_low, out_weight, preferred_element_type=jnp.float32) + jnp.dot(
        activated, fc_out_weight, preferred_element_type=jnp.float32
    )
    branches = lax.psum(partial_sum.astype(jnp.bfloat16), "tp").astype(jnp.float32)
    block_out = (inputs + branches + fc_out_bias).astype(jnp.bfloat16)[None]
    grad_out = cotangent[0]
    grad_float = grad_out.astype(jnp.float32)
    inputs_again, grad_float = lax.optimization_barrier((inputs, grad_float))
    x_hat, inv_std, normed = normalize(inputs_again, ln_gain, ln_bias)
    queries, key_rows, value_rows = project(normed, qkv_weight, cosine, sine_table)
    key_all, value_all = (
        lax.all_gather(key_rows, "ctx", axis=0, tiled=True),
        lax.all_gather(value_rows, "ctx", axis=0, tiled=True),
    )
    hidden_pre = jnp.dot(normed, fc_in_weight, preferred_element_type=jnp.float32) + fc_in_bias
    activated = gelu_tanh(hidden_pre).astype(jnp.bfloat16)
    scores = masked_scores(queries, key_all, own_places, key_places)
    row_max, row_total = softmax_parts(scores)
    probs_float = jnp.exp(scores - row_max) / row_total
    prob_low = probs_float.astype(jnp.bfloat16)
    attended = weigh_values(prob_low, value_all, head_count)
    attended_low = attended.reshape(row_count, local_width).astype(jnp.bfloat16)
    fc_out_bias_part = jnp.sum(grad_float, axis=0)
    fc_out_part = jnp.dot(activated.T, grad_out, preferred_element_type=jnp.float32)
    grad_act = jnp.dot(grad_out, fc_out_weight.T, preferred_element_type=jnp.float32)
    gelu_pull = jax.vjp(gelu_tanh, hidden_pre)[1]
    grad_hidden = gelu_pull(grad_act)[0].astype(jnp.bfloat16)
    fc_in_bias_part = jnp.sum(grad_hidden, axis=0, dtype=jnp.float32)
    fc_in_part = jnp.dot(normed.T, grad_hidden, preferred_element_type=jnp.float32)
    grad_normed = jnp.dot(grad_hidden, fc_in_weight.T, preferred_element_type=jnp.float32)
    out_part = jnp.dot(attended_low.T, grad_out, preferred_element_type=jnp.float32)
    grad_attended = (
        jnp.dot(grad_out, out_weight.T, preferred_element_type=jnp.float32)
        .astype(jnp.bfloat16)
        .reshape(row_count, head_count, HD)
    )
    key_three = key_all.reshape(key_all.shape[0], head_count, HD)
    value_three = value_all.reshape(value_all.shape[0], head_count, HD)
    grad_probs = jnp.einsum(
        "qhd,khd->hqk", grad_attended, value_three, preferred_element_type=jnp.float32
    )
    delta = jnp.einsum("qhd,qhd->hq", grad_attended.astype(jnp.float32), attended)[..., None]
    grad_scores = (probs_float * (grad_probs - delta)).astype(jnp.bfloat16)
    grad_query = (
        jnp.einsum("hqk,khd->qhd", grad_scores, key_three, preferred_element_type=jnp.float32)
        * score_scale
    )
    term_rows = row_count * lax.axis_size("ctx")
    grad_keys = (
        jnp.einsum("hqk,qhd->khd", grad_scores, queries, preferred_element_type=jnp.float32)
        * score_scale
    )
    grad_values = jnp.einsum(
        "hqk,qhd->khd", prob_low, grad_attended, preferred_element_type=jnp.float32
    )
    key_grads = lax.psum_scatter(
        jnp.concatenate(
            [
                grad_keys.reshape(term_rows, local_width),
                grad_values.reshape(term_rows, local_width),
            ],
            axis=1,
        ).astype(jnp.bfloat16),
        "ctx",
        scatter_dimension=0,
        tiled=True,
    ).astype(jnp.float32)
    grad_q_raw = unrotate(grad_query, cosine, sine_table).reshape(row_count, local_width)
    grad_k_raw = unrotate(
        key_grads[:, :local_width].reshape(row_count, head_count, HD), cosine, sine_table
    ).reshape(row_count, local_width)
    grad_projected = jnp.concatenate(
        [grad_q_raw, grad_k_raw, key_grads[:, local_width:]], axis=1
    ).astype(jnp.bfloat16)
    flat_weight = qkv_weight.reshape(model_width, 3 * local_width)
    qkv_part = jnp.dot(normed.T, grad_projected, preferred_element_type=jnp.float32).reshape(
        model_width, 3, local_width
    )
    grad_normed = grad_normed + jnp.dot(
        grad_projected, flat_weight.T, preferred_element_type=jnp.float32
    )
    grad_full = lax.psum(grad_normed.astype(jnp.bfloat16), "tp").astype(jnp.float32)
    grad_input, gain_part, bias_part = norm_back(grad_full, x_hat, inv_std, ln_gain)
    tokens_grad = (grad_float + grad_input)[None]
    (
        gain_grad,
        bias_grad,
        qkv_grad,
        out_grad,
        fc_in_grad,
        fc_in_bias_grad,
        fc_out_grad,
        fc_out_bias_grad,
    ) = lax.psum(
        (
            gain_part,
            bias_part,
            qkv_part,
            out_part,
            fc_in_part,
            fc_in_bias_part,
            fc_out_part,
            fc_out_bias_part,
        ),
        ("seq", "ctx"),
    )
    return (
        block_out,
        tokens_grad,
        gain_grad,
        bias_grad,
        qkv_grad,
        out_grad,
        fc_in_grad,
        fc_in_bias_grad,
        fc_out_grad,
        fc_out_bias_grad,
    )


def solution(mesh):
    placed = (
        P("seq", "ctx", None),
        P("seq", "ctx"),
        P("seq", "ctx", None),
        P(),
        P(),
        P(None, None, "tp"),
        P("tp", None),
        P(None, "tp"),
        P("tp"),
        P("tp", None),
        P(),
    )
    return jax.shard_map(
        local,
        mesh=mesh,
        in_specs=placed,
        out_specs=(
            P("seq", "ctx", None),
            P("seq", "ctx", None),
            P(),
            P(),
            P(None, None, "tp"),
            P("tp", None),
            P(None, "tp"),
            P("tp"),
            P("tp", None),
            P(),
        ),
        check_vma=False,
    )
```

profile of v0, /device:TPU:1, one launch (start us, length us, event | category | flops | bytes accessed | tf_op | source)
XLA Modules:
  0.0 1562.2 jit_solution(13140585687603578577)
XLA Ops:
  10.2 4.8 copy.39
  17.1 2.9 fusion.107
  25.2 3.0 fusion.52
  45.8 20.8 %all_gather.18 = s32[1,2048]{1,0:T(1,128)S(1)} all-gather(s32[1,256]{1,0:T(1,128)} %param.12), channel_id=1, replica_groups=mesh['seq'=8,'ctx'=8,'tp'=2] {'ctx'}, dimensions={1}, use_global_device_ids=true | all-gather | bytes 9216 | tf_op jit(solution)/shard_map/all_gather | solution.py:120
  69.3 30.3 %all-gather.9.cloned.1.call-done = bf16[2048,512]{0,1:T(8,128)(2,1)} async-done(((bf16[256,512]{0,1:T(8,128)(2,1)}), bf16[2048,512]{0,1:T(8,128)(2,1)}) %all-gather.9.cloned.1.call-update) | async-done | bytes 2097168 | tf_op jit(solution)/shard_map/all_gather | solution.py:146
  99.6 9.7 fusion.80
  109.3 21.3 %fusion.105 = (f32[8,256]{1,0:T(8,128)S(1)}, f32[8,256,2048]{2,1,0:T(8,128)}) fusion(f32[8,256,2048]{2,1,0:T(8,128)} %fusion.80, pred[256,2048]{1,0:T(8,128)(4,1)S(1)} %broadcast_compare_fusion), kind=kOutput, calls=%fused_computation.175 | output fusion | flops 25167872 | bytes 34086912 | tf_op jit(solution)/shard_map/sub | solution.py:153
  130.6 9.7 fusion.11
  140.2 15.6 all-gather.11.cloned.1.call-done
  155.8 2.9 copy.54
  158.8 8.2 fusion.54
  166.9 8.3 multiply_convert_fusion
  184.8 3.6 convolution_add_fusion
  188.5 3.0 convert_reduce_fusion
  193.7 4.8 fusion.44
  198.5 7.5 fusion.49
  206.0 6.1 fusion.32
  213.0 3.3 copy.40
  216.3 54.4 %all-gather.7.cloned.1.call-done = bf16[2048,512]{0,1:T(8,128)(2,1)} async-done(((bf16[256,512]{0,1:T(8,128)(2,1)}), bf16[2048,512]{0,1:T(8,128)(2,1)}) %all-gather.7.cloned.1.call-update) | async-done | bytes 2097168 | tf_op jit(solution)/shard_map/all_gather | solution.py:125
  270.8 9.8 fusion.76
  280.5 21.5 %fusion.104 = (f32[8,256]{1,0:T(8,128)S(1)}, f32[8,256,2048]{2,1,0:T(8,128)}) fusion(f32[8,256,2048]{2,1,0:T(8,128)} %fusion.76, pred[256,2048]{1,0:T(8,128)(4,1)} %copy-done.32), kind=kOutput, calls=%fused_computation.174 | output fusion | flops 25167872 | bytes 34086912 | tf_op jit(solution)/shard_map/sub | solution.py:130
  302.1 8.8 fusion.33
  312.1 46.3 %reduce-scatter.2.cloned.1.call-done = bf16[256,1024]{0,1:T(8,128)(2,1)} async-done(((bf16[2048,1024]{0,1:T(8,128)(2,1)}), bf16[256,1024]{0,1:T(8,128)(2,1)}) %reduce-scatter.2.cloned.1.call-update) | async-done | bytes 524304 | tf_op jit(solution)/shard_map/reduce_scatter | solution.py:190
  363.0 4.7 fusion.108
  369.5 3.7 fusion.75
  373.2 36.4 %all-reduce.8.cloned.1.call-done = (bf16[256,1024]{1,0:T(8,128)(2,1)}, bf16[256,1024]{1,0:T(8,128)(2,1)}) async-done(((bf16[256,1024]{1,0:T(8,128)(2,1)}, bf16[256,1024]{1,0:T(8,128)(2,1)}), (bf16[256,1024]{1,0:T(8,128)(2,1)}, bf16[256,1024]{1,0:T(8,128)(2,1)})) %all-reduce.8.cloned.1.call-update) | async-done | bytes 1048592 | tf_op jit(solution)/shard_map/psum | solution.py:138
  411.3 2.7 fusion.101
  414.1 326.1 %all-reduce = (f32[1024]{0:T(1024)}, f32[1024]{0:T(1024)}, f32[2048]{0:T(1024)}, f32[1024]{0:T(1024)}) all-reduce(f32[1024]{0:T(1024)S(1)} %get-tuple-element.24, f32[1024]{0:T(1024)S(1)} %get-tuple-element.27, f32[2048]{0:T(1024)S(1)} %copy-done.45, ...), channel_id=1, replica_groups=mesh['seq'=8,'ctx'=8,'tp'=2] {'seq','ctx'}, use_global_device_ids=true, to_apply=%region_14.15 | all-reduce | flops 5120 | bytes 40960 | tf_op jit(solution)/shard_map/psum | solution.py:228
  741.2 793.9 %all-reduce.6.cloned.1.call-done = (f32[1024,3,512]{0,2,1:T(8,128)}, f32[512,1024]{1,0:T(8,128)}, f32[1024,2048]{1,0:T(8,128)}, f32[2048,1024]{1,0:T(8,128)}) async-done(((f32[1024,3,512]{0,2,1:T(8,128)}, f32[512,1024]{1,0:T(8,128)}, f32[1024,2048]{1,0:T(8,128)}, f32[2048,1024]{1,0:T(8,128)}), (f32[1024,3,512]{0,2,1:T(8,128)}, f32[512,1024]{1,0:T(8,128)}, f32[1024,2048]{1,0:T(8,128)}, ...) | async-done | bytes 25165840 | tf_op jit(solution)/shard_map/psum | solution.py:228
  1535.1 6.7 copy.62
  1543.1 8.6 copy.86
  1551.7 3.4 copy.87
  (212 shorter events, 54.3 us)
Async XLA Ops:
  7.2 60.5 %copy-start = (bf16[512,1024]{1,0:T(8,128)(2,1)S(1)}, bf16[512,1024]{1,0:T(8,128)(2,1)}, u32[]{:S(2)}) copy-start(bf16[512,1024]{1,0:T(8,128)(2,1)} %param.17) | copy-start | bytes 3145732
  7.2 92.4 %all-gather.9.cloned.1.call-start = ((), (), s32[]{:S(2)}) async-start(), calls=%async_computation.3 | async-start | bytes 2359296 | tf_op jit(solution)/shard_map/all_gather | solution.py:146
  9.7 6.9 copy-start.2
  35.3 9.7 copy-start.17
  39.6 116.2 %all-gather.11.cloned.1.call-start = ((), (), s32[]{:S(2)}) async-start(), calls=%async_computation.4 | async-start | bytes 2359296 | tf_op jit(solution)/shard_map/all_gather | solution.py:147
  41.5 171.5 %all-gather.5.cloned.1.call-start = ((), (), s32[]{:S(2)}) async-start(), calls=%async_computation.1 | async-start | bytes 2359296 | tf_op jit(solution)/shard_map/all_gather | solution.py:126
  43.3 227.5 %all-gather.7.cloned.1.call-start = ((), (), s32[]{:S(2)}) async-start(), calls=%async_computation.2 | async-start | bytes 2359296 | tf_op jit(solution)/shard_map/all_gather | solution.py:125
  45.8 312.7 %reduce-scatter.2.cloned.1.call-start = ((), (), s32[]{:S(2)}) async-start(), calls=%async_computation.5 | async-start | bytes 4718592 | tf_op jit(solution)/shard_map/reduce_scatter | solution.py:190
  67.7 41.6 %copy-start.32 = (pred[256,2048]{1,0:T(8,128)(4,1)}, pred[256,2048]{1,0:T(8,128)(4,1)S(1)}, u32[]{:S(2)}) copy-start(pred[256,2048]{1,0:T(8,128)(4,1)S(1)} %broadcast_compare_fusion) | copy-start | bytes 1572868
  69.3 40.0 %copy-start.18 = (bf16[256,8,32]{0,2,1:T(8,128)(2,1)}, bf16[256,8,32]{0,2,1:T(8,128)(2,1)S(1)}, u32[]{:S(2)}) copy-start(bf16[256,8,32]{0,2,1:T(8,128)(2,1)S(1)} %copy.71) | copy-start | bytes 393220
  130.6 9.7 copy-start.44
  158.7 8.2 copy-start.8
  158.8 19.9 %slice-start = ((s8[8388608]{0:T(1024)(128)(4,1)}), s8[4194304]{0:T(1024)(128)(4,1)S(1)}, s32[]{:S(2)}) async-start(s8[8388608]{0:T(1024)(128)(4,1)} %bitcast.119), calls=%async_computation.8 | async-start | bytes 8388608
  166.9 8.3 copy-start.19
  166.9 11.7 slice-start.1
  182.9 226.8 %all-reduce.8.cloned.1.call-start = ((), (), s32[]{:S(2)}) async-start(), calls=%async_computation.7 | async-start | bytes 2097152 | tf_op jit(solution)/shard_map/psum | solution.py:138
  198.5 7.5 copy-start.4
  302.1 8.8 copy-start.23
  310.8 49.1 %copy-start.35 = (f32[256,16]{0,1:T(8,128)S(1)}, f32[256,16]{0,1:T(8,128)}, u32[]{:S(2)}) copy-start(f32[256,16]{0,1:T(8,128)} %get-tuple-element.68) | copy-start | bytes 49156
  312.1 48.1 %copy-start.34 = (bf16[256,8,32]{0,2,1:T(8,128)(2,1)S(1)}, bf16[256,8,32]{0,2,1:T(8,128)(2,1)}, u32[]{:S(2)}) copy-start(bf16[256,8,32]{0,2,1:T(8,128)(2,1)} %slice.204) | copy-start | bytes 393220
  362.7 1172.3 %all-reduce.6.cloned.1.call-start = ((), (), s32[]{:S(2)}) async-start(), calls=%async_computation.6 | async-start | bytes 50331648 | tf_op jit(solution)/shard_map/psum | solution.py:228
  373.2 36.5 %copy-start.3 = (f32[256,1024]{1,0:T(8,128)S(1)}, f32[256,1024]{1,0:T(8,128)}, u32[]{:S(2)}) copy-start(f32[256,1024]{1,0:T(8,128)} %copy-done.2) | copy-start | bytes 3145732
  373.2 36.5 %copy-start.38 = (f32[1024]{0:T(1024)S(1)}, f32[1024]{0:T(1024)}, u32[]{:S(2)}) copy-start(f32[1024]{0:T(1024)} %param.14) | copy-start | bytes 12292
  373.2 36.5 %copy-start.40 = (f32[256]{0:T(256)S(1)}, f32[256]{0:T(256)}, u32[]{:S(2)}) copy-start(f32[256]{0:T(256)} %copy-done.39) | copy-start | bytes 3076
  373.2 36.5 %copy-start.42 = (f32[256]{0:T(256)S(1)}, f32[256]{0:T(256)}, u32[]{:S(2)}) copy-start(f32[256]{0:T(256)} %copy-done.41) | copy-start | bytes 3076
  373.2 40.9 %copy-start.45 = (f32[2048]{0:T(1024)S(1)}, f32[2048]{0:T(1024)}, u32[]{:S(2)}) copy-start(f32[2048]{0:T(1024)} %get-tuple-element.77) | copy-start | bytes 24580
  373.2 367.0 %copy-start.7 = (bf16[1,256,1024]{2,1,0:T(8,128)(2,1)S(1)}, bf16[1,256,1024]{2,1,0:T(8,128)(2,1)}, u32[]{:S(2)}) copy-start(bf16[1,256,1024]{2,1,0:T(8,128)(2,1)} %param.11) | copy-start | bytes 1572868
  373.2 367.0 %copy-start.48 = (f32[1024]{0:T(1024)S(1)}, f32[1024]{0:T(1024)}, u32[]{:S(2)}) copy-start(f32[1024]{0:T(1024)} %param.21) | copy-start | bytes 12292
  409.7 330.6 %copy-start.31 = (bf16[256,1024]{1,0:T(8,128)(2,1)S(1)}, bf16[256,1024]{1,0:T(8,128)(2,1)}, u32[]{:S(2)}) copy-start(bf16[256,1024]{1,0:T(8,128)(2,1)} %get-tuple-element.36) | copy-start | bytes 1572868
  1535.1 6.7 copy-start.16
  1541.8 9.9 slice-start.2
  1543.1 8.6 slice-start.3
  (36 other events, 112.6 us)
Sparse Core Ops, SparseCore 0:
  39.7 59.7 all-gather.8
  102.5 53.3 all-gather.10
  158.1 53.7 all-gather.4
  214.0 56.7 all-gather.6
  275.1 83.3 reduce-scatter.1
  362.8 46.7 all-reduce.7
  413.8 1121.2 all-reduce.5
where the time goes:
time: 1570 us; the launch traced here: 1560 us
  waiting for transfers between devices  977 us (62%)
  blocking collectives  347 us (22%)
  matrix products  94.6 us (6%)
  other arithmetic  72.7 us (5%)
  local copies, waits for them, and re-layouts  55.1 us (4%)
    psum x1, waiting for transfers between devices, local(): lax.psum((gain_part, bias_part, qkv_part, out_part, fc_in_part, fc_in_bia...  794 us
    psum x1, blocking collectives, local(): lax.psum((gain_part, bias_part, qkv_part, out_part, fc_in_part, fc_in_bia...  326 us
    all_gather x2, waiting for transfers between devices, local(): lax.all_gather(key_rows, 'ctx', axis=0, tiled=True)  84.7 us
    reduce_scatter x1, waiting for transfers between devices, local(): lax.psum_scatter(jnp.concatenate([grad_keys.reshape(term_rows, local_widt...  46.3 us
    psum x1, waiting for transfers between devices, local(): lax.psum(partial_sum.astype(jnp.bfloat16), 'tp').astype(jnp.float32)  36.4 us
  transfers between devices with their start and end apart: 7, of which 6 were waited for; matrix products, arithmetic and copies ran while one was open for 11% of the time, Pallas kernels for 0%

commit v1 on v0

v1 whole, which is shorter than its diff:
```python
import math
from types import SimpleNamespace

import jax
import jax.numpy as jnp
from jax import lax
from jax.experimental import pallas as pl
from jax.experimental.pallas import tpu as pltpu
from jax.sharding import PartitionSpec as P

HD = 64
ROT = 32
T = 256
D = 1024
L = 512
F = 2048
MESH = pl.DeviceIdType.MESH
BF = jnp.bfloat16
F32 = jnp.float32
EPS = 1e-05
SIZES = (512, 256, 128, 64, 32)
OFFS = (0, 512, 768, 896, 960)


def dot(a, b):
    return lax.dot_general(a, b, (((1,), (0,)), ((), ())), preferred_element_type=F32)


def dot_nt(a, b):
    return lax.dot_general(a, b, (((1,), (1,)), ((), ())), preferred_element_type=F32)


def xor(a, b):
    return a + b - 2 * a * b


class Place:
    def __init__(self):
        seq, ctx, tp = lax.axis_index("seq"), lax.axis_index("ctx"), lax.axis_index("tp")
        self.seq, self.ctx, self.tp = seq, ctx, tp
        self.z, self.core, self.x, self.yh = seq // 2, seq % 2, ctx // 2, ctx % 2
        c, x, z = self.core, self.x, self.z
        flip = lambda i: i + 1 - 2 * (i % 2)
        self.sib = (z * 2 + 1 - c, ctx, tp)
        self.other_tp = (seq, ctx, 1 - tp)
        self.y = (seq, x * 2 + 1 - self.yh, tp)
        self.x_one = (seq, flip(x) * 2 + self.yh, tp)
        self.x_three = (seq, (3 - x) * 2 + self.yh, tp)
        self.z_one = (flip(z) * 2 + c, ctx, tp)
        self.z_three = ((3 - z) * 2 + c, ctx, tp)
        pick = lambda a, b: tuple((1 - c) * p + c * q for p, q in zip(a, b))
        u, v = (1 - c) * x + c * z, (1 - c) * z + c * x
        u_one, u_three = pick(self.x_one, self.z_one), pick(self.x_three, self.z_three)
        v_one, v_three = pick(self.z_one, self.x_one), pick(self.z_three, self.x_three)
        u0, u1, v0, v1 = u % 2, u // 2, v % 2, v // 2
        partner = (
            (u_one, u_three, v_one, v_three, self.y),
            (u_three, u_one, v_three, v_one, self.y),
        )
        bits = (
            (xor(u0, u1), u1, xor(v0, v1), v1, self.yh),
            (u1, u0, v1, v0, self.yh),
        )
        self.partner = partner
        self.keep, self.give = [], []
        for half in range(2):
            base, keep, give = 0, [], []
            for step in range(5):
                size, bit = SIZES[step], bits[half][step]
                keep.append(pl.multiple_of(base + bit * size, 32))
                give.append(pl.multiple_of(base + (1 - bit) * size, 32))
                base = base + bit * size
            self.keep.append(keep)
            self.give.append(give)


def remote(src, dst, send, recv, device):
    return pltpu.make_async_remote_copy(
        src_ref=src, dst_ref=dst, send_sem=send, recv_sem=recv, device_id=device, device_id_type=MESH
    )


def rotate(u, cosine, even, odd):
    return u * cosine + pltpu.roll(u, 127, 1) * even + pltpu.roll(u, 1, 1) * odd


def layer_kernel(
    pos, tok_h, cot_h, gain, lnb, wqkv_h, wout_h, fin_h, finb, fout_h, foutb,
    out_b, out_t, out_s, out_r,
    tok, cot, nrm, xhat, inv, wqkv, wout, fin, fout, tabs,
    send1, land1, ptile, pland, psm, qg, kv, kvt, sbuf, pbuf, dkv, aq,
    send2, land2, act_o, act_b, gh_o, gh_b, lf_o, lf_b, nrm_t, cot_t, act_t,
    branch, gnp, tps, tpl, g0, g1, g2, l0, l1, l2, r0, r1, r2, vs, vw,
    in_sem, sib_s, sib_r, a_s, a_r, p_s, p_r, b_s, b_r, tp_s, tp_r,
    rs_s, rs_r, ag_s, ag_r, fw_s, fw_r, st_s, v_s, v_r, ps_sem,
):
    me = Place()
    core, ctx = me.core, me.ctx
    g, lands, res = (g0, g1, g2), (l0, l1, l2), (r0, r1, r2)

    loads = [
        pltpu.make_async_copy(a, b, in_sem.at[i])
        for i, (a, b) in enumerate(
            ((tok_h, tok), (cot_h, cot.at[0]), (wqkv_h, wqkv), (wout_h, wout), (fin_h, fin), (fout_h, fout))
        )
    ]
    for copy in loads:
        copy.start()

    barrier = pltpu.get_barrier_semaphore()
    peers = [(me.seq, lax.rem(ctx + k, 8), me.tp) for k in range(1, 8)]
    for device in peers + [me.sib, me.other_tp, me.z_one, me.z_three]:
        pl.semaphore_signal(barrier, inc=1, device_id=device, device_id_type=MESH)

    first = pos[0, 0]
    lane = lax.broadcasted_iota(jnp.int32, (T, 128), 1)
    row = lax.broadcasted_iota(jnp.int32, (T, 128), 0)
    in_head = lane % HD
    freq = jnp.exp((in_head // 2).astype(F32) * (-2.0 * math.log(10000.0) / ROT))
    theta = (row + first).astype(F32) * freq
    turning = in_head < ROT
    sine = jnp.where(turning, jnp.sin(theta), 0.0)
    tabs[0] = jnp.where(turning, jnp.cos(theta), 1.0)
    tabs[1] = jnp.where(lane % 2 == 0, -sine, 0.0)
    tabs[2] = jnp.where(lane % 2 == 0, 0.0, sine)
    ptile[...] = jnp.full((8, 128), first, jnp.int32)

    loads[0].wait()

    def norm_rows(i, _):
        rows = pl.ds(pl.multiple_of(i * 64, 64), 64)
        x = tok[rows, :].astype(F32)
        x = x - jnp.mean(x, axis=-1, keepdims=True)
        inv_std = lax.rsqrt(jnp.mean(x * x, axis=-1, keepdims=True) + EPS)
        x = x * inv_std
        xhat[rows, :] = x
        inv[rows, :] = jnp.broadcast_to(inv_std, (64, 128))
        nrm[0, rows, :] = (x * gain[...] + lnb[...]).astype(BF)
        return 0

    lax.fori_loop(0, T // 64, norm_rows, 0)

    loads[1].wait()
    pl.semaphore_wait(barrier, 11)
    sib = [None] * 5
    sib[0] = remote(cot.at[0], cot.at[1], sib_s.at[0], sib_r.at[0], me.sib)
    sib[1] = remote(nrm.at[0], nrm.at[1], sib_s.at[1], sib_r.at[1], me.sib)
    sib[0].start()
    sib[1].start()

    loads[2].wait()
    loads[3].wait()
    normed = nrm[0]
    low_lane = lane < HD

    def lanes(e):
        return slice(128 * e, 128 * e + 128)

    for e in range(4):
        cols = slice(128 * e, 128 * e + 128)
        turn = (tabs[0], tabs[1], tabs[2])
        q = rotate(dot(normed, wqkv[0, :, cols]), *turn) * HD ** (-0.5)
        k = rotate(dot(normed, wqkv[1, :, cols]), *turn)
        v = dot(normed, wqkv[2, :, cols])
        ga = dot_nt(cot[0], wout[128 * e : 128 * e + 128, :])
        swap = lambda a: pltpu.roll(a, HD, 1)
        send1[2 * e, :, 0:128] = jnp.where(low_lane, q, swap(ga)).astype(BF)
        send1[2 * e, :, 128:256] = jnp.where(low_lane, k, swap(v)).astype(BF)
        send1[2 * e + 1, :, 0:128] = jnp.where(low_lane, swap(q), ga).astype(BF)
        send1[2 * e + 1, :, 128:256] = jnp.where(low_lane, swap(k), v).astype(BF)
    first_out, place_out = [], []
    for k in range(1, 8):
        to = lax.rem(ctx + k, 8)
        place_out.append(remote(ptile, pland.at[ctx], p_s.at[k - 1], p_r.at[k - 1], peers[k - 1]))
        first_out.append(remote(send1.at[to], land1.at[ctx], a_s.at[k - 1], a_r.at[k - 1], peers[k - 1]))
    for copy in place_out + first_out:
        copy.start()
    land1[ctx] = send1[ctx]
    pland[ctx] = ptile[...]

    loads[4].wait()
    loads[5].wait()
    vs[0] = jnp.zeros((8, D), F32)

    def hidden(half, act_ref, gh_ref, i):
        start = pl.multiple_of(half * 1024 + i * 256, 256)
        here = pl.ds(pl.multiple_of(i * 256, 256), 256)
        u = dot(nrm[0], fin[:, pl.ds(start, 256)]) + finb[:, pl.ds(start, 256)]
        z = math.sqrt(2.0 / math.pi) * (u + 0.044715 * u * u * u)
        t = jnp.tanh(z)
        act_ref[:, here] = (0.5 * u * (1.0 + t)).astype(BF)
        slope = 0.5 * (1.0 + t) + (0.5 * math.sqrt(2.0 / math.pi)) * u * (1.0 - t * t) * (
            1.0 + 3 * 0.044715 * u * u
        )
        grad = dot_nt(cot[0], fout[pl.ds(start, 256), :]) * slope
        low = grad.astype(BF)
        gh_ref[:, here] = low
        vs[0, pl.ds(2 + half, 1), here] = jnp.sum(low.astype(F32), axis=0, keepdims=True)

    def other_half(i, _):
        hidden(1 - core, act_o, gh_o, i)
        return 0

    def own_half(i, _):
        hidden(core, act_b.at[0], gh_b.at[0], i)
        return 0

    lax.fori_loop(0, 4, other_half, 0)
    sib[2] = remote(act_o, act_b.at[1], sib_s.at[2], sib_r.at[2], me.sib)
    sib[3] = remote(gh_o, gh_b.at[1], sib_s.at[3], sib_r.at[3], me.sib)
    sib[2].start()
    sib[3].start()
    lax.fori_loop(0, 4, own_half, 0)
    vs[0, 4:5, :] = jnp.sum(cot[0].astype(F32), axis=0, keepdims=True)

    sib[0].wait_recv()
    sib[1].wait_recv()

    def turn_over(src, dst):
        def body(i, _):
            here = pl.ds(pl.multiple_of(i * 128, 128), 128)
            for token in range(2):
                dst[here, token * T : token * T + T] = src[token, :, here].T
            return 0

        lax.fori_loop(0, D // 128, body, 0)

    turn_over(nrm, nrm_t)
    turn_over(cot, cot_t)
    sib[2].wait_recv()
    turn_over(act_b, act_t)

    def outer(left_t, right, dest):
        def body(i, _):
            rows = pl.ds(pl.multiple_of(i * 128, 128), 128)
            a0, a1 = left_t[rows, 0:T], left_t[rows, T : 2 * T]
            for half in range(2):
                b = slice(512 * half, 512 * half + 512)
                dest[half, rows, :] = (dot(a0, right[0, :, b]) + dot(a1, right[1, :, b])).astype(BF)
            return 0

        lax.fori_loop(0, D // 128, body, 0)

    def rs_copy(m, h, s):
        return remote(
            g[m].at[h, pl.ds(me.give[h][s], SIZES[s])],
            lands[m].at[h, pl.ds(OFFS[s], SIZES[s])],
            rs_s.at[m, h, s],
            rs_r.at[m, h, s],
            me.partner[h][s],
        )

    def ag_copy(m, h, s):
        rows = pl.ds(me.keep[h][s], SIZES[s])
        return remote(
            res[m].at[h, rows], res[m].at[h, rows], ag_s.at[m, h, s], ag_r.at[m, h, s], me.partner[h][s]
        )

    def fw_copy(m, h, s):
        rows = pl.ds((me.keep if s == 0 else me.give)[h][0], SIZES[0])
        return remote(
            res[m].at[h, rows], out_r.at[m, core, h, rows], fw_s.at[m, h, s], fw_r.at[m, h, s], me.sib
        )

    def st_copy(m, h, s):
        rows = pl.ds((me.keep if s == 0 else me.give)[h][0], SIZES[0])
        return pltpu.make_async_copy(res[m].at[h, rows], out_r.at[m, core, h, rows], st_s.at[m, h, s])

    def rs_start(m):
        for h in range(2):
            rs_copy(m, h, 0).start()

    def rs_step(m, s):
        size = SIZES[s]
        block = min(size, 64)
        for h in range(2):
            rs_copy(m, h, s).wait_recv()

            def body(i, _):
                here = pl.ds(pl.multiple_of(me.keep[h][s] + i * block, 32), block)
                there = pl.ds(pl.multiple_of(OFFS[s] + i * block, 32), block)
                total = g[m][h, here, :].astype(F32) + lands[m][h, there, :].astype(F32)
                (g if s < 4 else res)[m][h, here, :] = total.astype(BF)
                return 0

            lax.fori_loop(0, size // block, body, 0)
            if s < 4:
                rs_copy(m, h, s + 1).start()
            else:
                ag_copy(m, h, 4).start()

    def ag_step(m, s):
        for h in range(2):
            ag_copy(m, h, s).wait_recv()
            if s > 0:
                ag_copy(m, h, s - 1).start()
            if s == 1:
                fw_copy(m, h, 0).start()
                st_copy(m, h, 0).start()
            if s == 0:
                fw_copy(m, h, 1).start()
                st_copy(m, h, 1).start()

    outer(act_t, cot, g0)
    rs_start(0)
    sib[3].wait_recv()
    outer(nrm_t, gh_b, g1)
    rs_start(1)

    for copy in place_out:
        copy.wait_recv()
    to_scalar = pltpu.make_async_copy(pland, psm, ps_sem)
    to_scalar.start()
    for copy in first_out:
        copy.wait_recv()
    to_scalar.wait()
    rank = [psm[c, 0, 0] // T for c in range(8)]
    for r in range(8):
        at = 0
        for c in range(8):
            at = jnp.where(rank[c] == r, c, at)
        block = land1[at]
        rows = slice(r * T, r * T + T)
        qg[rows, :] = block[:, 0:128]
        kv[rows, :] = block[:, 128:256]
        kvt[:, rows] = block[:, 128:256].T

    dkv[...] = jnp.zeros_like(dkv)

    def attend(r):
        qgr = qg[r * T : r * T + T, :]
        zero = jnp.zeros_like(qgr)
        lower = lax.broadcasted_iota(jnp.int32, (T, 128), 1) < HD
        q = jnp.where(lower, qgr, zero)
        ga = jnp.where(lower, zero, qgr)
        ga_t = qgr.T[HD:, :].astype(F32)

        def key(j):
            return pl.ds(pl.multiple_of(j * T, T), T)

        def scores(j, top):
            s = dot_nt(kv[key(j), :], q)
            sbuf[key(j), :] = s
            return jnp.maximum(top, jnp.max(s.reshape(T // 8, 8, T), axis=0))

        top = lax.fori_loop(0, r, scores, jnp.full((8, T), -1e30, F32))
        s = dot_nt(kv[key(r), :], q)
        below = lax.broadcasted_iota(jnp.int32, (T, T), 0) <= lax.broadcasted_iota(jnp.int32, (T, T), 1)
        s = jnp.where(below, s, -1e30)
        sbuf[key(r), :] = s
        top = jnp.maximum(top, jnp.max(s.reshape(T // 8, 8, T), axis=0))
        top = jnp.max(top, axis=0, keepdims=True)

        def expo(j, total):
            e = jnp.exp(sbuf[key(j), :] - top)
            sbuf[key(j), :] = e
            return total + jnp.sum(e.reshape(T // 8, 8, T), axis=0)

        total = lax.fori_loop(0, r + 1, expo, jnp.zeros((8, T), F32))
        scale = 1.0 / jnp.sum(total, axis=0, keepdims=True)

        def weigh(j, att):
            prob = (sbuf[key(j), :] * scale).astype(BF)
            pbuf[key(j), :] = prob
            return att + dot(kvt[HD:, key(j)], prob)

        att = lax.fori_loop(0, r + 1, weigh, jnp.zeros((HD, T), F32))
        delta = jnp.sum(ga_t * att, axis=0, keepdims=True)

        def back(j, dq):
            dp = dot_nt(kv[key(j), :], ga)
            ds = (sbuf[key(j), :] * scale * (dp - delta)).astype(BF)
            dkv[key(j), :] += dot(ds, q) + dot(pbuf[key(j), :], ga)
            return dq + dot(kvt[:HD, key(j)], ds)

        dq = lax.fori_loop(0, r + 1, back, jnp.zeros((HD, T), F32))
        both = jnp.concatenate([att, dq * HD ** (-0.5)], axis=0)
        aq[r, :, 0:128] = both.T.astype(BF)
        aq[r, :, 128:256] = dkv[r * T : r * T + T, :].astype(BF)

    attend(7)
    attend(6)
    rs_step(0, 0)
    attend(5)
    rs_step(1, 0)
    attend(4)
    rs_step(0, 1)
    attend(3)
    rs_step(1, 1)
    rs_step(0, 2)
    attend(2)
    rs_step(1, 2)
    rs_step(0, 3)
    attend(1)
    attend(0)

    for c in range(8):
        send2[c] = aq[rank[c]]
    second_out = []
    for k in range(1, 8):
        to = lax.rem(ctx + k, 8)
        second_out.append(remote(send2.at[to], land2.at[ctx], b_s.at[k - 1], b_r.at[k - 1], peers[k - 1]))
    for copy in second_out:
        copy.start()
    land2[ctx] = send2[ctx]
    rs_step(1, 3)
    rs_step(0, 4)
    rs_step(1, 4)

    own, oth = pl.multiple_of(core * 1024, 1024), pl.multiple_of((1 - core) * 1024, 1024)

    def mixed(i, _):
        cols = pl.ds(pl.multiple_of(i * 256, 256), 256)
        branch[:, cols] = dot(act_b[0], fout[pl.ds(own, 1024), cols]) + dot(act_o[...], fout[pl.ds(oth, 1024), cols])
        gnp[:, cols] = dot_nt(gh_b[0], fin[cols, pl.ds(own, 1024)]) + dot_nt(gh_o[...], fin[cols, pl.ds(oth, 1024)])
        return 0

    lax.fori_loop(0, 4, mixed, 0)
    ag_step(0, 4)
    ag_step(1, 4)
    ag_step(0, 3)
    ag_step(1, 3)

    for copy in second_out:
        copy.wait_recv()

    def gather_heads(half, ref):
        for e in range(2):
            here = slice(128 * e, 128 * e + 128)
            low, high = 4 * half + 2 * e, 4 * half + 2 * e + 1
            t0, t1 = land2[low, :, 0:128].astype(F32), land2[high, :, 0:128].astype(F32)
            t2, t3 = land2[low, :, 128:256].astype(F32), land2[high, :, 128:256].astype(F32)
            swap = lambda a: pltpu.roll(a, HD, 1)
            turn = (tabs[0], -tabs[1], -tabs[2])
            att = jnp.where(low_lane, t0, swap(t1))
            dq = rotate(jnp.where(low_lane, swap(t0), t1), *turn)
            dk = rotate(jnp.where(low_lane, t2, swap(t3)), *turn)
            dv = jnp.where(low_lane, swap(t2), t3)
            for j, part in enumerate((dq, dk, dv, att)):
                ref[:, 256 * j + 128 * e : 256 * j + 128 * e + 128] = part.astype(BF)

    gather_heads(1 - core, lf_o)
    sib[4] = remote(lf_o, lf_b.at[1], sib_s.at[4], sib_r.at[4], me.sib)
    sib[4].start()
    gather_heads(core, lf_b.at[0])

    def late(i, _):
        cols = pl.ds(pl.multiple_of(i * 256, 256), 256)
        part, grad = branch[:, cols], gnp[:, cols]
        for ref, half in ((lf_b.at[0], core), (lf_o, 1 - core)):
            at = pl.multiple_of(half * 256, 256)
            part = part + dot(ref[:, 768:1024], wout[pl.ds(at, 256), cols])
            for j in range(3):
                grad = grad + dot_nt(ref[:, 256 * j : 256 * j + 256], wqkv[j, cols, pl.ds(at, 256)])
        tps[0, :, cols] = part.astype(BF)
        tps[1, :, cols] = grad.astype(BF)
        vs[0, 0:1, cols] = jnp.sum(grad * xhat[:, cols], axis=0, keepdims=True)
        vs[0, 1:2, cols] = jnp.sum(grad, axis=0, keepdims=True)
        return 0

    lax.fori_loop(0, 4, late, 0)
    tp_copy = [remote(tps.at[i], tpl.at[i], tp_s.at[i], tp_r.at[i], me.other_tp) for i in range(2)]
    for copy in tp_copy:
        copy.start()

    v_to = (me.sib, me.x_one, me.x_three, me.z_one, me.z_three, me.y, me.other_tp)

    def v_copy(i):
        return remote(vs.at[i], vw.at[i], v_s.at[i], v_r.at[i], v_to[i])

    def v_step(i):
        v_copy(i).wait_recv()
        total = vs[i] + vw[i]
        if i == 6:
            keep = lax.broadcasted_iota(jnp.int32, (8, D), 0) < 2
            out_s[...] = jnp.where(keep, total, vs[i])
        else:
            vs[i + 1] = total
            v_copy(i + 1).start()

    v_copy(0).start()

    sib[4].wait_recv()

    def last_outer(i, _):
        rows = pl.ds(pl.multiple_of(i * 128, 128), 128)
        a0, a1 = nrm_t[rows, 0:T], nrm_t[rows, T : 2 * T]
        c0, c1 = cot_t[rows, 0:T], cot_t[rows, T : 2 * T]
        g2[0, rows, :] = (dot(a0, lf_b[0, :, 0:512]) + dot(a1, lf_b[1, :, 0:512])).astype(BF)
        g2[1, rows, 0:256] = (dot(a0, lf_b[0, :, 512:768]) + dot(a1, lf_b[1, :, 512:768])).astype(BF)
        g2[1, rows, 256:512] = (dot(c0, lf_b[0, :, 768:1024]) + dot(c1, lf_b[1, :, 768:1024])).astype(BF)
        return 0

    lax.fori_loop(0, 8, last_outer, 0)
    rs_start(2)
    v_step(0)
    ag_step(0, 2)
    ag_step(1, 2)
    v_step(1)
    rs_step(2, 0)
    v_step(2)
    ag_step(0, 1)
    ag_step(1, 1)
    rs_step(2, 1)
    v_step(3)
    rs_step(2, 2)
    v_step(4)

    tp_copy[0].wait_recv()
    tp_copy[1].wait_recv()

    def finish(i, _):
        rows = pl.ds(pl.multiple_of(i * 32, 32), 32)
        branches = tps[0, rows, :].astype(F32) + tpl[0, rows, :].astype(F32)
        out_b[rows, :] = (tok[rows, :].astype(F32) + branches.astype(BF).astype(F32) + foutb[...]).astype(BF)
        grad = (tps[1, rows, :].astype(F32) + tpl[1, rows, :].astype(F32)).astype(BF).astype(F32)
        scaled = grad * gain[...]
        x = xhat[rows, :]
        mean_one = jnp.mean(scaled, axis=-1, keepdims=True)
        mean_two = jnp.mean(scaled * x, axis=-1, keepdims=True)
        inv_std = inv[rows, 0:1]
        out_t[rows, :] = cot[0, rows, :].astype(F32) + inv_std * (scaled - mean_one - x * mean_two)
        return 0

    lax.fori_loop(0, T // 32, finish, 0)
    rs_step(2, 3)
    v_step(5)
    rs_step(2, 4)
    v_step(6)
    ag_step(0, 0)
    ag_step(1, 0)
    for s in range(4, -1, -1):
        ag_step(2, s)

    for m in range(3):
        for h in range(2):
            for s in range(2):
                fw_copy(m, h, s).wait()
                st_copy(m, h, s).wait()
            for s in range(5):
                rs_copy(m, h, s).wait_send()
                ag_copy(m, h, s).wait_send()
    for copy in sib + place_out + first_out + second_out + tp_copy:
        copy.wait_send()
    for i in range(7):
        v_copy(i).wait_send()


def call_layer(*args):
    anyspace = pl.BlockSpec(memory_space=pl.ANY)
    vmem = pl.BlockSpec(memory_space=pltpu.VMEM)
    smem = pl.BlockSpec(memory_space=pltpu.SMEM)
    dma = lambda *shape: pltpu.SemaphoreType.DMA(shape)
    V = pltpu.VMEM
    return pl.pallas_call(
        layer_kernel,
        name="layer",
        out_shape=(
            jax.ShapeDtypeStruct((T, D), BF),
            jax.ShapeDtypeStruct((T, D), F32),
            jax.ShapeDtypeStruct((8, D), F32),
            jax.ShapeDtypeStruct((3, 2, 2, 1024, 512), BF),
        ),
        in_specs=[smem, anyspace, anyspace, vmem, vmem, anyspace, anyspace, anyspace, vmem, anyspace, vmem],
        out_specs=(vmem, vmem, vmem, anyspace),
        scratch_shapes=[
            V((T, D), BF), V((2, T, D), BF), V((2, T, D), BF), V((T, D), F32), V((T, 128), F32),
            V((3, D, L), BF), V((L, D), BF), V((D, F), BF), V((F, D), BF), V((3, T, 128), F32),
            V((8, T, 256), BF), V((8, T, 256), BF), V((8, 128), jnp.int32), V((8, 8, 128), jnp.int32),
            pltpu.SMEM((8, 8, 128), jnp.int32),
            V((8 * T, 128), BF), V((8 * T, 128), BF), V((128, 8 * T), BF),
            V((8 * T, T), F32), V((8 * T, T), BF), V((8 * T, 128), F32), V((8, T, 256), BF),
            V((8, T, 256), BF), V((8, T, 256), BF),
            V((T, 1024), BF), V((2, T, 1024), BF), V((T, 1024), BF), V((2, T, 1024), BF),
            V((T, 1024), BF), V((2, T, 1024), BF),
            V((D, 2 * T), BF), V((D, 2 * T), BF), V((1024, 2 * T), BF),
            V((T, D), F32), V((T, D), F32), V((2, T, D), BF), V((2, T, D), BF),
            V((2, 1024, 512), BF), V((2, 1024, 512), BF), V((2, 1024, 512), BF),
            V((2, 992, 512), BF), V((2, 992, 512), BF), V((2, 992, 512), BF),
            V((2, 1024, 512), BF), V((2, 1024, 512), BF), V((2, 1024, 512), BF),
            V((7, 8, D), F32), V((7, 8, D), F32),
            dma(6), dma(5), dma(5), dma(7), dma(7), dma(7), dma(7), dma(7), dma(7), dma(2), dma(2),
            dma(3, 2, 5), dma(3, 2, 5), dma(3, 2, 5), dma(3, 2, 5),
            dma(3, 2, 2), dma(3, 2, 2), dma(3, 2, 2), dma(7), dma(7), pltpu.SemaphoreType.DMA(()),
        ],
        compiler_params=pltpu.CompilerParams(
            collective_id=0, has_side_effects=True, vmem_limit_bytes=62 * 2**20
        ),
    )(*args)


def widen_kernel(a, b, c, d, fc_out, fc_in, qkv, out):
    for half in range(2):
        fc_out[:, 512 * half : 512 * half + 512] = a[0, 0, half].astype(F32)
    for core in range(2):
        for half in range(2):
            start = 1024 * core + 512 * half
            fc_in[:, start : start + 512] = b[0, core, half].astype(F32)
        here = slice(256 * core, 256 * core + 256)
        qkv[0, :, here] = c[0, core, 0, :, 0:256].astype(F32)
        qkv[1, :, here] = c[0, core, 0, :, 256:512].astype(F32)
        qkv[2, :, here] = c[0, core, 1, :, 0:256].astype(F32)
    out[...] = d[0, 0, 0].astype(F32).T


def call_widen(grads):
    n = 8
    spec = pl.BlockSpec
    return pl.pallas_call(
        widen_kernel,
        name="widen",
        grid=(n,),
        in_specs=[
            spec((1, 1, 2, 2048 // n, 512), lambda i: (0, i // (n // 2), 0, i % (n // 2), 0)),
            spec((1, 2, 2, 1024 // n, 512), lambda i: (1, 0, 0, i, 0)),
            spec((1, 2, 2, 1024 // n, 512), lambda i: (2, 0, 0, i, 0)),
            spec((1, 1, 1, 1024, 128), lambda i: (2, i // 4, 1, 0, 2 + i // 2 % 2)),
        ],
        out_specs=(
            spec((2048 // n, 1024), lambda i: (i, 0)),
            spec((1024 // n, 2048), lambda i: (i, 0)),
            spec((3, 1024 // n, 512), lambda i: (0, i, 0)),
            spec((128, 1024), lambda i: (i // 2, 0)),
        ),
        out_shape=(
            jax.ShapeDtypeStruct((F, D), F32),
            jax.ShapeDtypeStruct((D, F), F32),
            jax.ShapeDtypeStruct((3, D, L), F32),
            jax.ShapeDtypeStruct((L, D), F32),
        ),
        compiler_params=pltpu.CompilerParams(vmem_limit_bytes=60 * 2**20),
    )(grads, grads, grads, grads)


def local(
    tokens, positions, cotangent, ln_gain, ln_bias, qkv_weight, out_weight,
    fc_in_weight, fc_in_bias, fc_out_weight, fc_out_bias,
):
    block_out, tokens_grad, small, grads = call_layer(
        positions,
        tokens[0],
        cotangent[0],
        ln_gain[None],
        ln_bias[None],
        qkv_weight.transpose(1, 0, 2),
        out_weight,
        fc_in_weight,
        fc_in_bias[None],
        fc_out_weight,
        fc_out_bias[None],
    )
    fc_out_grad, fc_in_grad, qkv_grad, out_grad = call_widen(grads)
    return (
        block_out[None],
        tokens_grad[None],
        small[0],
        small[1],
        qkv_grad.transpose(1, 0, 2),
        out_grad,
        fc_in_grad,
        small[2:4].reshape(F),
        fc_out_grad,
        small[4],
    )


def solution(mesh):
    placed = (
        P("seq", "ctx", None), P("seq", "ctx"), P("seq", "ctx", None), P(), P(),
        P(None, None, "tp"), P("tp", None), P(None, "tp"), P("tp"), P("tp", None), P(),
    )
    return jax.shard_map(
        local,
        mesh=mesh,
        in_specs=placed,
        out_specs=(
            P("seq", "ctx", None), P("seq", "ctx", None), P(), P(), P(None, None, "tp"),
            P("tp", None), P(None, "tp"), P("tp"), P("tp", None), P(),
        ),
        check_vma=False,
    )
```

time: 1570 us -> 170 us (0.11)
  waiting for transfers between devices: 977 us -> 0 us
  blocking collectives: 347 us -> 0 us
  Pallas kernels: 0 us -> 164 us
  matrix products: 94.6 us -> 0 us
  other arithmetic: 72.7 us -> 0 us
  local copies, waits for them, and re-layouts: 55.1 us -> 4.61 us
    psum x2 -> x0, waiting for transfers between devices: 830 us -> none  [the longest x1 794 us: local(): lax.psum((gain_part, bias_part, qkv_part, out_part, fc_in_part, fc_in_bia...]
    psum x1 -> x0, blocking collectives: 326 us -> none  [local(): lax.psum((gain_part, bias_part, qkv_part, out_part, fc_in_part, fc_in_bia...]
    pallas_call x0 -> x2, Pallas kernels: none -> 164 us  [the longest x1 150 us: call_layer(): pl.pallas_call(layer_kernel, name='layer', out_shape=(jax.ShapeDtypeStruc...]
    all_gather x4 -> x0, waiting for transfers between devices: 100 us -> none  [the longest x2 84.7 us: local(): lax.all_gather(key_rows, 'ctx', axis=0, tiled=True)]
    dot_general x21 -> x0, matrix products: 94.6 us -> none  [the longest x2 19.5 us: masked_scores(): jnp.einsum('qhd,khd->hqk', queries, key_three, preferred_element_type=jnp...]
    reduce_scatter x1 -> x0, waiting for transfers between devices: 46.3 us -> none  [local(): lax.psum_scatter(jnp.concatenate([grad_keys.reshape(term_rows, local_widt...]
    sub x2 -> x0, other arithmetic: 42.8 us -> none  [the longest x1 21.5 us: local(): prob_low = (jnp.exp(scores - row_max) / row_total).astype(jnp.bfloat16)]
    unnamed x129 -> x8, local copies, waits for them, and re-layouts: 30.2 us -> 3.14 us
  transfers between devices with their start and end apart: 7 -> 0, of which waited for: 6 -> 0; matrix products, arithmetic and copies ran while one was open for 11% -> 0% of each run, Pallas kernels for 0% -> 0%
where the time goes in v1:
time: 170 us
  Pallas kernels  164 us (96%)
  local copies, waits for them, and re-layouts  4.61 us (3%)
    pallas_call x1, Pallas kernels, call_layer(): pl.pallas_call(layer_kernel, name='layer', out_shape=(jax.ShapeDtypeStruc...  150 us
    pallas_call x1, Pallas kernels, call_widen(): pl.pallas_call(widen_kernel, name='widen', grid=(n,), in_specs=[spec((1,...  14.5 us

profile of v1, /device:TPU:1, one launch (start us, length us, event | category | flops | bytes accessed | tf_op | source)
XLA Modules:
  0.0 169.5 jit_solution(2760037468959974904)
XLA Ops:
  0.6 149.7 %layer.1 = (bf16[256,1024]{1,0:T(8,128)(2,1)}, f32[256,1024]{1,0:T(8,128)}, f32[8,1024]{1,0:T(8,128)}, bf16[3,2,2,1024,512]{4,3,2,1,0:T(8,128)(2,1)}) custom-call(s32[1,256]{1,0:T(1,128)} %pos.1, bf16[256,1024]{1,0:T(8,128)(2,1)} %bitcast.20, bf16[256,1024]{1,0:T(8,128)(2,1)} %bitcast.21, f32[1,1024]{1,0:T(1,128)} %bitcast.25, f32[1,1024]{1,0:T(1,128)} %bitcast.26, ...), custom_call_target="tpu_custom_call" | custom-call | tf_op jit(solution)/shard_map/layer/pallas_call | solution.py:555
  150.4 0.8 slice_bitcast_fusion
  151.1 1.5 fusion
  152.6 0.6 copy.23
  153.2 0.0 copy-start.1
  153.2 0.0 copy-start
  153.2 14.5 %widen.1 = (f32[2048,1024]{1,0:T(8,128)}, f32[1024,2048]{1,0:T(8,128)}, f32[3,1024,512]{2,1,0:T(8,128)}, f32[512,1024]{1,0:T(8,128)}) custom-call(bf16[3,2,2,1024,512]{4,3,2,1,0:T(8,128)(2,1)} %get-tuple-element.21.a.b.c.d, bf16[3,2,2,1024,512]{4,3,2,1,0:T(8,128)(2,1)} %get-tuple-element.21.a.b.c.d, bf16[3,2,2,1024,512]{4,3,2,1,0:T(8,128)(2,1)} %get-tuple-element.21.a.b.c.d, ...), custom_call_target="tpu_custom_call" | custom-call | tf_op jit(solution)/shard_map/widen/pallas_call | solution.py:609
  167.8 0.0 copy-done.1
  167.8 0.8 copy.26
  168.6 0.0 copy-done
  168.6 1.0 copy.27
Async XLA Ops:
  153.2 14.6 %copy-start.1 = (bf16[256,1024]{1,0:T(8,128)(2,1)S(1)}, bf16[256,1024]{1,0:T(8,128)(2,1)}, u32[]{:S(2)}) copy-start(bf16[256,1024]{1,0:T(8,128)(2,1)} %get-tuple-element.18) | copy-start | bytes 1572868
  153.2 15.4 %copy-start = (f32[256,1024]{1,0:T(8,128)S(1)}, f32[256,1024]{1,0:T(8,128)}, u32[]{:S(2)}) copy-start(f32[256,1024]{1,0:T(8,128)} %get-tuple-element.19) | copy-start | bytes 3145732

commit v2 on v1

v2 whole, which is shorter than its diff:
```python
import math
from types import SimpleNamespace

import jax
import jax.numpy as jnp
from jax import lax
from jax.experimental import pallas as pl
from jax.experimental.pallas import tpu as pltpu
from jax.sharding import PartitionSpec as P

HD = 64
ROT = 32
T = 256
D = 1024
L = 512
F = 2048
MESH = pl.DeviceIdType.MESH
BF = jnp.bfloat16
F32 = jnp.float32
EPS = 1e-05
ROWS = (1024, 1024, 1024, 512)
WIDE = (512, 512, 384, 256)
ORDER = ("xz", "xz", "xz", "xz")


def dot(a, b):
    return lax.dot_general(a, b, (((1,), (0,)), ((), ())), preferred_element_type=F32)


def dot_nt(a, b):
    return lax.dot_general(a, b, (((1,), (1,)), ((), ())), preferred_element_type=F32)


def xor(a, b):
    return a + b - 2 * a * b


class Place:
    def __init__(self):
        seq, ctx, tp = lax.axis_index("seq"), lax.axis_index("ctx"), lax.axis_index("tp")
        self.seq, self.ctx, self.tp = seq, ctx, tp
        self.z, self.core, self.x, self.yh = seq // 2, seq % 2, ctx // 2, ctx % 2
        c, x, z = self.core, self.x, self.z
        flip = lambda i: i + 1 - 2 * (i % 2)
        self.sib = (z * 2 + 1 - c, ctx, tp)
        self.other_tp = (seq, ctx, 1 - tp)
        self.y = (seq, x * 2 + 1 - self.yh, tp)
        self.x_one = (seq, flip(x) * 2 + self.yh, tp)
        self.x_three = (seq, (3 - x) * 2 + self.yh, tp)
        self.z_one = (flip(z) * 2 + c, ctx, tp)
        self.z_three = ((3 - z) * 2 + c, ctx, tp)
        c = {"xz": c, "z": 1, "x": 0}
        self.order = [Order(self, c[kind]) for kind in ORDER]


class Order:
    def __init__(self, me, c):
        x, z = me.x, me.z
        pick = lambda a, b: tuple((1 - c) * p + c * q for p, q in zip(a, b))
        u, v = (1 - c) * x + c * z, (1 - c) * z + c * x
        one, three = pick(me.x_one, me.z_one), pick(me.x_three, me.z_three)
        self.before, self.after = (one, three), (three, one)
        u0, u1 = u % 2, u // 2
        w0 = 1 - u0
        self.keep = (2 * xor(u0, u1) + u1, 2 * u1 + u0)
        self.give = (2 * xor(u0, u1) + 1 - u1, 2 * u1 + 1 - u0)
        self.their_give = (2 * xor(w0, u1) + 1 - u1, 2 * (1 - u1) + u0)
        self.their_keep = (2 * xor(w0, u1) + u1, 2 * (1 - u1) + 1 - u0)
        self.place = v * 2 + me.yh
        self.others = []
        for k in range(1, 8):
            to = lax.rem(self.place + k, 8)
            there = to // 2
            zz, xx = (1 - c) * there + c * z, (1 - c) * x + c * there
            self.others.append((to, (zz * 2 + me.core, xx * 2 + to % 2, me.tp)))


def remote(src, dst, send, recv, device):
    return pltpu.make_async_remote_copy(
        src_ref=src, dst_ref=dst, send_sem=send, recv_sem=recv, device_id=device, device_id_type=MESH
    )


def rotate(u, cosine, even, odd):
    return u * cosine + pltpu.roll(u, 127, 1) * even + pltpu.roll(u, 1, 1) * odd


def keys(j):
    return slice(j * T, j * T + T)


def tri(r):
    return r * (r + 1) // 2 * T


def layer_kernel(
    pos_h, tok_h, cot_h, gain, lnb, wqkv_h, wout_h, fin_h, finb, fout_h, foutb,
    out_b, out_t, out_s, out_0, out_1, out_2, out_3,
    pos, tok, cot, nrm, xhat, inv, wqkv, wout, fin, fout, tabs, send1, land1, ptile, pland, psm, qg, kv,
    kvt, sbuf, pbuf, atts, aq, send2, land2, sib_att, send3, land3, act_o, act_b, gh_o, gh_b, lf_o, lf_b,
    nrm_t, tps, tpl, g0, g1, g2, g3, l0, l1, l2, l3, r0, r1, r2, r3, t0, t1, t2, t3, w0, w1, w2, w3, vs,
    vw, blk, tgr, in_sem, sib_s, sib_r, all_s, all_r, tp_s, tp_r, rs_s, rs_r, fw_s, fw_r, st_s, v_s, v_r,
    o_s,
):
    me = Place()
    core, ctx = me.core, me.ctx
    g, lands, res, outs = (g0, g1, g2, g3), (l0, l1, l2, l3), (r0, r1, r2, r3), (out_0, out_1, out_2, out_3)
    slots, whole_q = (t0, t1, t2, t3), (w0, w1, w2, w3)

    loads = [
        pltpu.make_async_copy(a, b, in_sem.at[i])
        for i, (a, b) in enumerate(
            (
                (pos_h, pos), (tok_h, tok), (cot_h, cot.at[0]), (wqkv_h, wqkv), (wout_h, wout),
                (fin_h, fin), (fout_h, fout),
            )
        )
    ]
    for copy in loads:
        copy.start()

    barrier = pltpu.get_barrier_semaphore()
    peers = [(me.seq, lax.rem(ctx + k, 8), me.tp) for k in range(1, 8)]
    across = [
        ((lax.rem(me.z + k, 4) * 2 + core, me.x * 2 + yh, me.tp)) for k in range(1, 4) for yh in range(2)
    ]
    for device in peers + across + [me.sib, me.other_tp]:
        pl.semaphore_signal(barrier, inc=1, device_id=device, device_id_type=MESH)

    loads[0].wait()
    first = pos[0, 0]
    lane = lax.broadcasted_iota(jnp.int32, (T, 128), 1)
    row = lax.broadcasted_iota(jnp.int32, (T, 128), 0)
    in_head = lane % HD
    low_lane = lane < HD
    freq = jnp.exp((in_head // 2).astype(F32) * (-2.0 * math.log(10000.0) / ROT))
    theta = (row + first).astype(F32) * freq
    turning = in_head < ROT
    sine = jnp.where(turning, jnp.sin(theta), 0.0)
    tabs[0] = jnp.where(turning, jnp.cos(theta), 1.0)
    tabs[1] = jnp.where(lane % 2 == 0, -sine, 0.0)
    tabs[2] = jnp.where(lane % 2 == 0, 0.0, sine)
    ptile[...] = jnp.full((8, 128), first, jnp.int32)

    loads[1].wait()

    def norm_rows(i, _):
        rows = pl.ds(pl.multiple_of(i * 64, 64), 64)
        x = tok[rows, :].astype(F32)
        x = x - jnp.mean(x, axis=-1, keepdims=True)
        inv_std = lax.rsqrt(jnp.mean(x * x, axis=-1, keepdims=True) + EPS)
        x = x * inv_std
        xhat[rows, :] = x
        inv[rows, :] = jnp.broadcast_to(inv_std, (64, 128))
        nrm[0, rows, :] = (x * gain[...] + lnb[...]).astype(BF)
        return 0

    lax.fori_loop(0, T // 64, norm_rows, 0)

    loads[2].wait()
    pl.semaphore_wait(barrier, 15)

    sib_pairs = (
        (cot.at[0], cot.at[1]),
        (nrm.at[0], nrm.at[1]),
        (act_o, act_b.at[1]),
        (gh_o, gh_b.at[1]),
        (land2.at[pl.ds(4 * (1 - core), 4)], sib_att),
        (lf_o, lf_b.at[1]),
    )

    def to_sib(i):
        return remote(*sib_pairs[i], sib_s.at[i], sib_r.at[i], me.sib)

    def to_all(src, dst, i):
        for k in range(1, 8):
            to = lax.rem(ctx + k, 8)
            here = src if i == 0 else src.at[to]
            remote(here, dst.at[ctx], all_s.at[i], all_r.at[i], peers[k - 1]).start()
        dst[ctx] = src[...] if i == 0 else src[ctx]

    def all_seven(dst, i):
        return remote(dst.at[pl.ds(0, 7)], dst.at[pl.ds(0, 7)], all_s.at[i], all_r.at[i], me.sib)

    to_sib(0).start()
    to_sib(1).start()

    loads[3].wait()
    loads[4].wait()
    to_all(ptile, pland, 0)
    normed = nrm[0]
    swap = lambda a: pltpu.roll(a, HD, 1)
    for e in range(4):
        cols = slice(128 * e, 128 * e + 128)
        turn = (tabs[0], tabs[1], tabs[2])
        q = rotate(dot(normed, wqkv[0, :, cols]), *turn) * HD ** (-0.5)
        k = rotate(dot(normed, wqkv[1, :, cols]), *turn)
        v = dot(normed, wqkv[2, :, cols])
        ga = dot_nt(cot[0], wout[cols, :])
        send1[2 * e, :, 0:128] = jnp.where(low_lane, q, swap(ga)).astype(BF)
        send1[2 * e, :, 128:256] = jnp.where(low_lane, k, swap(v)).astype(BF)
        send1[2 * e + 1, :, 0:128] = jnp.where(low_lane, swap(q), ga).astype(BF)
        send1[2 * e + 1, :, 128:256] = jnp.where(low_lane, swap(k), v).astype(BF)
    to_all(send1, land1, 1)

    loads[5].wait()
    loads[6].wait()
    vs[0] = jnp.zeros((8, D), F32)

    def hidden(half, act_ref, gh_ref, i):
        start = pl.multiple_of(half * 1024 + i * 256, 256)
        here = pl.ds(pl.multiple_of(i * 256, 256), 256)
        u = dot(nrm[0], fin[:, pl.ds(start, 256)]) + finb[:, pl.ds(start, 256)]
        z = math.sqrt(2.0 / math.pi) * (u + 0.044715 * u * u * u)
        t = jnp.tanh(z)
        act_ref[:, here] = (0.5 * u * (1.0 + t)).astype(BF)
        slope = 0.5 * (1.0 + t) + (0.5 * math.sqrt(2.0 / math.pi)) * u * (1.0 - t * t) * (
            1.0 + 3 * 0.044715 * u * u
        )
        grad = dot_nt(cot[0], fout[pl.ds(start, 256), :]) * slope
        low = grad.astype(BF)
        gh_ref[:, here] = low
        vs[0, pl.ds(2 + half, 1), here] = jnp.sum(low.astype(F32), axis=0, keepdims=True)

    def other_half(i, _):
        hidden(1 - core, act_o, gh_o, i)
        return 0

    def own_half(i, _):
        hidden(core, act_b.at[0], gh_b.at[0], i)
        return 0

    lax.fori_loop(0, 4, other_half, 0)
    to_sib(2).start()
    to_sib(3).start()
    lax.fori_loop(0, 4, own_half, 0)

    def turn_over(src, dst):
        def body(i, _):
            here = pl.ds(pl.multiple_of(i * 128, 128), 128)
            for token in range(2):
                dst[token, here, :] = src[token, :, here].T
            return 0

        lax.fori_loop(0, D // 128, body, 0)

    def quarter(m, q):
        return pl.ds(pl.multiple_of(q * (ROWS[m] // 4), ROWS[m] // 4), ROWS[m] // 4)

    def swap_copy(m, h, k):
        o = me.order[m]
        q = (o.their_give, o.their_keep, o.give)[k][h]
        device = o.after[h] if k == 2 else o.before[h]
        return remote(g[m].at[h, quarter(m, q)], lands[m].at[k, h], rs_s.at[m, 0], rs_r.at[m, min(k, 1)], device)

    def arrived(m, ref, i):
        remote(ref, ref, rs_s.at[m, 0], rs_r.at[m, i], me.sib).wait_recv()

    def add(m, h, into, rows, start, *terms):
        block = 64

        def body(i, _):
            here = pl.ds(pl.multiple_of(i * block, block), block)
            total = g[m][h, pl.ds(pl.multiple_of(start + i * block, block), block), :].astype(F32)
            for k in terms:
                total = total + lands[m][k, h, here, :].astype(F32)
            if into is None:
                g[m][h, pl.ds(pl.multiple_of(start + i * block, block), block), :] = total.astype(BF)
            else:
                lands[m][into, h, here, :] = total.astype(BF)
            return 0

        lax.fori_loop(0, rows // block, body, 0)

    def first_sum(m):
        arrived(m, lands[m].at[0], 0)
        for h in range(2):
            add(m, h, None, ROWS[m] // 4, me.order[m].give[h] * (ROWS[m] // 4), 0)
            swap_copy(m, h, 2).start()

    def second_sum(m):
        arrived(m, lands[m].at[pl.ds(1, 2)], 1)
        for h in range(2):
            add(m, h, 2, ROWS[m] // 4, me.order[m].keep[h] * (ROWS[m] // 4), 1, 2)
        o, n = me.order[m], ROWS[m] // 32
        for to, device in o.others:
            piece = lands[m].at[2, :, pl.ds(pl.multiple_of(to * n, n), n)]
            remote(piece, slots[m].at[o.place], rs_s.at[m, 1], rs_r.at[m, 2], device).start()

    def third_sum(m):
        seven = slots[m].at[pl.ds(0, 7)]
        arrived(m, seven, 2)
        o, n = me.order[m], ROWS[m] // 32
        here = pl.ds(pl.multiple_of(o.place * n, n), n)
        slots[m][o.place] = lands[m][2, :, here, :]
        for h in range(2):
            total = slots[m][0, h].astype(F32)
            for k in range(1, 8):
                total = total + slots[m][k, h].astype(F32)
            whole_q[m][h, here, :] = total.astype(BF)
        piece = whole_q[m].at[:, here]
        for to, device in o.others:
            remote(piece, piece, rs_s.at[m, 2], rs_r.at[m, 3], device).start()

    def hand_over(m, h, src, q):
        there = outs[m].at[core, h, quarter(m, q)]
        remote(src, there, fw_s.at[m], fw_r.at[m], me.sib).start()
        pltpu.make_async_copy(src, there, st_s.at[m]).start()

    def spread(m, h, src, q, k):
        o = me.order[m]
        device = (o.before if k else o.after)[h]
        remote(src, res[m].at[h, quarter(m, q)], rs_s.at[m, 3], rs_r.at[m, 4 + k], device).start()

    def first_gather(m):
        arrived(m, slots[m].at[pl.ds(0, 7)], 3)
        o = me.order[m]
        for k in range(2):
            for h in range(2):
                spread(m, h, whole_q[m].at[h], o.keep[h], k)
        for h in range(2):
            hand_over(m, h, whole_q[m].at[h], o.keep[h])

    def second_gather(m):
        arrived(m, lands[m].at[0], 4)
        o = me.order[m]
        for h in range(2):
            src = res[m].at[h, quarter(m, o.give[h])]
            spread(m, h, src, o.give[h], 1)
            hand_over(m, h, src, o.give[h])

    def third_gather(m):
        arrived(m, lands[m].at[pl.ds(0, 2)], 5)
        o = me.order[m]
        for h in range(2):
            for q in (o.their_give[h], o.their_keep[h]):
                hand_over(m, h, res[m].at[h, quarter(m, q)], q)

    def outer(m, left_t, right):
        o = me.order[m]
        for k, qs in enumerate((o.their_give, o.their_keep, o.give, o.keep)):
            for h in range(2):
                rows = quarter(m, qs[h])
                cols = slice(WIDE[m] * h, WIDE[m] * h + WIDE[m])
                total = dot(left_t[0, rows, :], right[0, :, cols]) + dot(left_t[1, rows, :], right[1, :, cols])
                g[m][h, rows, :] = total.astype(BF)
                if k < 2:
                    swap_copy(m, h, k).start()

    act_t = pbuf.at[pl.ds(0, 2 * D)].reshape(2, D, T)
    to_sib(2).wait_recv()
    turn_over(act_b, act_t)
    to_sib(0).wait_recv()
    outer(0, act_t, cot)
    to_sib(1).wait_recv()
    turn_over(nrm, nrm_t)
    to_sib(3).wait_recv()
    outer(1, nrm_t, gh_b)
    vs[0, 4:5, :] = jnp.sum(cot[0].astype(F32), axis=0, keepdims=True)

    all_seven(pland, 0).wait_recv()
    to_scalar = pltpu.make_async_copy(pland, psm, o_s.at[2])
    to_scalar.start()
    all_seven(land1, 1).wait_recv()
    to_scalar.wait()
    rank = [psm[c, 0, 0] // T for c in range(8)]
    for r in range(8):
        at = 0
        for c in range(8):
            at = jnp.where(rank[c] == r, c, at)
        block = land1[at]
        qg[keys(r), :] = block[:, 0:128]
        kv[keys(r), :] = block[:, 128:256]
        kvt[:, keys(r)] = block[:, 128:256].T

    causal = lax.broadcasted_iota(jnp.int32, (T, T), 0) <= lax.broadcasted_iota(jnp.int32, (T, T), 1)
    deltas = [None] * 8

    def split(r):
        both_lanes = qg[keys(r), :]
        zero = jnp.zeros_like(both_lanes)
        return jnp.where(low_lane, both_lanes, zero), jnp.where(low_lane, zero, both_lanes)

    def scores(r):
        q, _ = split(r)
        top = jnp.full((8, T), -1e30, F32)
        for j in range(r + 1):
            s = dot_nt(kv[keys(j), :], q)
            if j == r:
                s = jnp.where(causal, s, -1e30)
            sbuf[r % 2, keys(j), :] = s
            top = jnp.maximum(top, jnp.max(s.reshape(T // 8, 8, T), axis=0))
        return top

    def weigh(r, top):
        top = jnp.max(top, axis=0, keepdims=True)
        total, att = jnp.zeros((8, T), F32), jnp.zeros((HD, T), F32)
        for j in range(r + 1):
            e = jnp.exp(sbuf[r % 2, keys(j), :] - top)
            total = total + jnp.sum(e.reshape(T // 8, 8, T), axis=0)
            low = e.astype(BF)
            pbuf[tri(r) + j * T : tri(r) + j * T + T, :] = low
            att = att + dot(kvt[HD:, keys(j)], low)
        scale = 1.0 / jnp.sum(total, axis=0, keepdims=True)
        att = att * scale
        atts[r] = att.astype(BF)
        both_lanes = qg[keys(r), :]
        ga_t = (both_lanes.T.astype(F32)[HD:, :] * scale).astype(BF)
        deltas[r] = jnp.sum(ga_t.astype(F32) * att, axis=0, keepdims=True)
        ga = jnp.concatenate([jnp.zeros((HD, T), BF), ga_t], axis=0).T
        qg[keys(r), :] = jnp.where(low_lane, both_lanes, ga)

    def back(r):
        q, ga = split(r)
        dq = jnp.zeros((HD, T), F32)
        for j in range(r + 1):
            prob = pbuf[tri(r) + j * T : tri(r) + j * T + T, :]
            dp = dot_nt(kv[keys(j), :], ga)
            ds = (prob.astype(F32) * (dp - deltas[r])).astype(BF)
            update = dot(ds, q) + dot(prob, ga)
            if r == 7:
                sbuf[0, keys(j), 0:128] = update
            else:
                sbuf[0, keys(j), 0:128] += update
            dq = dq + dot(kvt[:HD, keys(j)], ds)
        dq = (dq * HD ** (-0.5)).astype(BF)
        aq[r, 0:256, :] = sbuf[0, keys(r), 0:128].astype(BF)
        aq[r, 256:320, :] = dq[:, 0:128]
        aq[r, 320:384, :] = dq[:, 128:256]

    ahead = scores(7)
    for r in range(7, -1, -1):
        now = ahead
        if r:
            ahead = scores(r - 1)
        weigh(r, now)
    for c in range(8):
        send2[c] = atts[rank[c]]
    to_all(send2, land2, 2)
    back(7)
    back(6)
    back(5)
    first_sum(0)
    back(4)
    back(3)
    first_sum(1)
    back(2)
    back(1)
    back(0)
    for c in range(8):
        send3[c] = aq[rank[c]]
    to_all(send3, land3, 3)

    own, oth = pl.multiple_of(core * 1024, 1024), pl.multiple_of((1 - core) * 1024, 1024)
    all_seven(land2, 2).wait_recv()
    to_sib(4).start()
    att_rows = land2[...].reshape(L, T).T

    def branch(i, _):
        cols = pl.ds(pl.multiple_of(i * 256, 256), 256)
        part = dot(act_b[0], fout[pl.ds(own, 1024), cols]) + dot(act_o[...], fout[pl.ds(oth, 1024), cols])
        tps[0, i] = (part + dot(att_rows, wout[:, cols])).astype(BF)
        return 0

    lax.fori_loop(0, 4, branch, 0)

    def tp_copy(i, j):
        return remote(tps.at[i, j], tpl.at[i, j], tp_s.at[i], tp_r.at[i], me.other_tp)

    def tp_start(*which):
        for i, j in which:
            tp_copy(i, j).start()

    tp_start((0, 0), (0, 1), (0, 2), (0, 3))
    to_sib(4).wait_recv()
    mine = land2[pl.ds(4 * core, 4)].reshape(T, T)
    theirs = sib_att[...].reshape(T, T)
    for h in range(2):
        for q in range(2):
            cols = slice(512 * h + 256 * q, 512 * h + 256 * q + 256)
            g3[h, 256 * q : 256 * q + 256, :] = (dot(mine, cot[0, :, cols]) + dot(theirs, cot[1, :, cols])).astype(BF)
    for k in range(2):
        for h in range(2):
            swap_copy(3, h, k).start()

    def mixed(i, _):
        cols = pl.ds(pl.multiple_of(i * 256, 256), 256)
        sbuf[1, cols, :] = dot_nt(gh_b[0], fin[cols, pl.ds(own, 1024)]) + dot_nt(gh_o[...], fin[cols, pl.ds(oth, 1024)])
        return 0

    lax.fori_loop(0, 4, mixed, 0)
    second_sum(0)
    second_sum(1)
    third_sum(0)
    all_seven(land3, 3).wait_recv()

    def gather_heads(half, ref):
        for e in range(2):
            low, high = 4 * half + 2 * e, 4 * half + 2 * e + 1
            t0, t1 = land3[low, 0:256, :].astype(F32), land3[high, 0:256, :].astype(F32)
            dq_t = jnp.concatenate(
                [
                    jnp.concatenate([land3[i, 256:320, :], land3[i, 320:384, :]], axis=1)
                    for i in (low, high)
                ],
                axis=0,
            )
            turn = (tabs[0], -tabs[1], -tabs[2])
            dq = rotate(dq_t.T.astype(F32), *turn)
            dk = rotate(jnp.where(low_lane, t0, swap(t1)), *turn)
            dv = jnp.where(low_lane, swap(t0), t1)
            for j, part in enumerate((dq, dk, dv)):
                ref[:, 256 * j + 128 * e : 256 * j + 128 * e + 128] = part.astype(BF)

    gather_heads(1 - core, lf_o)
    to_sib(5).start()
    gather_heads(core, lf_b.at[0])
    third_sum(1)
    to_sib(5).wait_recv()
    outer(2, nrm_t, lf_b)

    def late(i, _):
        cols = pl.ds(pl.multiple_of(i * 256, 256), 256)
        grad = sbuf[1, cols, :]
        for ref, half in ((lf_b.at[0], core), (lf_o, 1 - core)):
            at = pl.multiple_of(half * 256, 256)
            for j in range(3):
                grad = grad + dot_nt(ref[:, 256 * j : 256 * j + 256], wqkv[j, cols, pl.ds(at, 256)])
        tps[1, i] = grad.astype(BF)
        vs[0, 0:1, cols] = jnp.sum(grad * xhat[:, cols], axis=0, keepdims=True)
        vs[0, 1:2, cols] = jnp.sum(grad, axis=0, keepdims=True)
        return 0

    lax.fori_loop(0, 4, late, 0)

    v_to = (me.sib, me.y, me.x_one, me.x_three, me.z_one, me.z_three, me.other_tp)

    def v_copy(i):
        return remote(vs.at[i], vw.at[i], v_s.at[0], v_r.at[i], v_to[i])

    def v_step(i):
        v_copy(i).wait_recv()
        total = vs[i] + vw[i]
        if i == 6:
            here = lax.broadcasted_iota(jnp.int32, (8, D), 0) < 2
            out_s[...] = jnp.where(here, total, vs[i])
        else:
            vs[i + 1] = total
            v_copy(i + 1).start()

    v_copy(0).start()

    def finish(i, _):
        rows = pl.ds(pl.multiple_of(i * 32, 32), 32)

        def whole(k):
            parts = [tps[k, j, rows, :].astype(F32) + tpl[k, j, rows, :].astype(F32) for j in range(4)]
            return jnp.concatenate(parts, axis=1).astype(BF).astype(F32)

        blk[rows, :] = (tok[rows, :].astype(F32) + whole(0) + foutb[...]).astype(BF)
        grad = whole(1)
        scaled = grad * gain[...]
        x = xhat[rows, :]
        mean_one = jnp.mean(scaled, axis=-1, keepdims=True)
        mean_two = jnp.mean(scaled * x, axis=-1, keepdims=True)
        inv_std = inv[rows, 0:1]
        tgr[rows, :] = cot[0, rows, :].astype(F32) + inv_std * (scaled - mean_one - x * mean_two)
        return 0

    to_out = [pltpu.make_async_copy(blk, out_b, o_s.at[0]), pltpu.make_async_copy(tgr, out_t, o_s.at[1])]

    def tp_all(i):
        return remote(tps.at[i], tpl.at[i], tp_s.at[i], tp_r.at[i], me.other_tp)

    first_sum(2)
    tp_start((1, 0), (1, 1))
    first_sum(3)
    first_gather(0)
    first_gather(1)
    second_sum(2)
    v_step(0)
    v_step(1)
    second_sum(3)
    third_sum(2)
    third_sum(3)
    first_gather(2)
    v_step(2)
    v_step(3)
    first_gather(3)
    second_gather(0)
    second_gather(1)
    tp_start((1, 2), (1, 3))
    v_step(4)
    second_gather(2)
    second_gather(3)
    v_step(5)
    third_gather(0)
    third_gather(1)
    v_step(6)
    tp_all(0).wait_recv()
    tp_all(1).wait_recv()
    lax.fori_loop(0, T // 32, finish, 0)
    to_out[0].start()
    to_out[1].start()
    third_gather(3)
    third_gather(2)
    for m in range(4):
        seven = slots[m].at[pl.ds(0, 7)]
        for i, ref in enumerate((lands[m], seven, seven, lands[m])):
            remote(ref, ref, rs_s.at[m, i], rs_r.at[m, 0], me.sib).wait_send()
        half_out = outs[m].at[1 - core]
        remote(res[m], half_out, fw_s.at[m], fw_r.at[m], me.sib).wait()
        pltpu.make_async_copy(res[m], outs[m].at[core], st_s.at[m]).wait()
    for i in range(6):
        to_sib(i).wait_send()
    all_seven(pland, 0).wait_send()
    all_seven(land1, 1).wait_send()
    all_seven(land2, 2).wait_send()
    all_seven(land3, 3).wait_send()
    for i in range(2):
        tp_all(i).wait_send()
        to_out[i].wait()
    remote(vs, vw, v_s.at[0], v_r.at[0], me.sib).wait_send()


def call_layer(*args):
    anyspace = pl.BlockSpec(memory_space=pl.ANY)
    vmem = pl.BlockSpec(memory_space=pltpu.VMEM)
    dma = lambda *shape: pltpu.SemaphoreType.DMA(shape)
    V = pltpu.VMEM
    return pl.pallas_call(
        layer_kernel,
        name="layer",
        out_shape=(
            jax.ShapeDtypeStruct((T, D), BF),
            jax.ShapeDtypeStruct((T, D), F32),
            jax.ShapeDtypeStruct((8, D), F32),
        )
        + tuple(jax.ShapeDtypeStruct((2, 2, ROWS[m], WIDE[m]), BF) for m in range(4)),
        in_specs=[anyspace] * 3 + [vmem, vmem, anyspace, anyspace, anyspace, vmem, anyspace, vmem],
        out_specs=(anyspace, anyspace, vmem) + (anyspace,) * 4,
        scratch_shapes=[
            pltpu.SMEM((1, T), jnp.int32), V((T, D), BF), V((2, T, D), BF), V((2, T, D), BF), V((T, D), F32),
            V((T, 128), F32), V((3, D, L), BF), V((L, D), BF), V((D, F), BF), V((F, D), BF), V((3, T, 128), F32),
            V((8, T, 256), BF), V((8, T, 256), BF), V((8, 128), jnp.int32), V((8, 8, 128), jnp.int32),
            pltpu.SMEM((8, 8, 128), jnp.int32), V((8 * T, 128), BF), V((8 * T, 128), BF), V((128, 8 * T), BF),
            V((2, 8 * T, T), F32), V((36 * T, T), BF), V((8, HD, T), BF), V((8, 384, 128), BF), V((8, HD, T), BF),
            V((8, HD, T), BF), V((4, HD, T), BF), V((8, 384, 128), BF), V((8, 384, 128), BF), V((T, 1024), BF),
            V((2, T, 1024), BF), V((T, 1024), BF), V((2, T, 1024), BF), V((T, 768), BF), V((2, T, 768), BF),
            V((2, D, T), BF), V((2, 4, T, T), BF), V((2, 4, T, T), BF), V((2, 1024, 512), BF),
            V((2, 1024, 512), BF), V((2, 1024, 384), BF), V((2, 512, 256), BF), V((3, 2, 256, 512), BF),
            V((3, 2, 256, 512), BF), V((3, 2, 256, 384), BF), V((3, 2, 128, 256), BF), V((2, 1024, 512), BF),
            V((2, 1024, 512), BF), V((2, 1024, 384), BF), V((2, 512, 256), BF), V((8, 2, 32, 512), BF),
            V((8, 2, 32, 512), BF), V((8, 2, 32, 384), BF), V((8, 2, 16, 256), BF), V((2, 256, 512), BF),
            V((2, 256, 512), BF), V((2, 256, 384), BF), V((2, 128, 256), BF), V((7, 8, D), F32), V((7, 8, D), F32),
            V((T, D), BF), V((T, D), F32), dma(7), dma(6), dma(6), dma(4), dma(4), dma(2), dma(2), dma(4, 4),
            dma(4, 6), dma(4), dma(4), dma(4), dma(1), dma(7), dma(3),
        ],
        compiler_params=pltpu.CompilerParams(
            collective_id=0, has_side_effects=True, vmem_limit_bytes=63 * 2**20
        ),
    )(*args)


def widen_kernel(
    a, b, c, d, block, grads, small,
    fc_out, fc_in, qkv, out, block_out, tokens_grad, gain, bias, fc_in_bias, fc_out_bias,
):
    for half in range(2):
        fc_out[:, 512 * half : 512 * half + 512] = a[0, half].astype(F32)
    for core in range(2):
        for half in range(2):
            start = 1024 * core + 512 * half
            fc_in[:, start : start + 512] = b[core, half].astype(F32)
        here = 256 * core
        qkv[0, :, here : here + 256] = c[core, 0, :, 0:256].astype(F32)
        qkv[1, :, here : here + 128] = c[core, 0, :, 256:384].astype(F32)
        qkv[1, :, here + 128 : here + 256] = c[core, 1, :, 0:128].astype(F32)
        qkv[2, :, here : here + 256] = c[core, 1, :, 128:384].astype(F32)
    for half in range(2):
        for part in range(2):
            start = 512 * half + 256 * part
            out[:, start : start + 256] = d[0, half, part].astype(F32)
    block_out[...] = block[...]
    tokens_grad[...] = grads[...]
    gain[...] = small[0:1, :]
    bias[...] = small[1:2, :]
    fc_in_bias[:, 0:1024] = small[2:3, :]
    fc_in_bias[:, 1024:2048] = small[3:4, :]
    fc_out_bias[...] = small[4:5, :]


def call_widen(block, grads, small, a, b, c, d):
    n = 8
    half = n // 2
    spec = pl.BlockSpec
    shape = jax.ShapeDtypeStruct
    return pl.pallas_call(
        widen_kernel,
        name="widen",
        grid=(n,),
        in_specs=[
            spec((1, 2, F // n, 512), lambda i: (i // half, 0, i % half, 0)),
            spec((2, 2, D // n, 512), lambda i: (0, 0, i, 0)),
            spec((2, 2, D // n, 384), lambda i: (0, 0, i, 0)),
            spec((1, 2, 2, L // n, 256), lambda i: (i // half, 0, 0, i % half, 0)),
            spec((T // n, D), lambda i: (i, 0)),
            spec((T // n, D), lambda i: (i, 0)),
            spec((8, D), lambda i: (0, 0)),
        ],
        out_specs=(
            spec((F // n, D), lambda i: (i, 0)),
            spec((D // n, F), lambda i: (i, 0)),
            spec((3, D // n, L), lambda i: (0, i, 0)),
            spec((L // n, D), lambda i: (i, 0)),
            spec((T // n, D), lambda i: (i, 0)),
            spec((T // n, D), lambda i: (i, 0)),
            spec((1, D), lambda i: (0, 0)),
            spec((1, D), lambda i: (0, 0)),
            spec((1, F), lambda i: (0, 0)),
            spec((1, D), lambda i: (0, 0)),
        ),
        out_shape=(
            shape((F, D), F32), shape((D, F), F32), shape((3, D, L), F32), shape((L, D), F32),
            shape((T, D), BF), shape((T, D), F32),
            shape((1, D), F32), shape((1, D), F32), shape((1, F), F32), shape((1, D), F32),
        ),
        compiler_params=pltpu.CompilerParams(vmem_limit_bytes=60 * 2**20),
    )(a, b, c, d.reshape(2, 2, 2, 256, 256), block, grads, small)


def local(
    tokens, positions, cotangent, ln_gain, ln_bias, qkv_weight, out_weight,
    fc_in_weight, fc_in_bias, fc_out_weight, fc_out_bias,
):
    parts = call_layer(
        positions,
        tokens[0],
        cotangent[0],
        ln_gain[None],
        ln_bias[None],
        qkv_weight.transpose(1, 0, 2),
        out_weight,
        fc_in_weight,
        fc_in_bias[None],
        fc_out_weight,
        fc_out_bias[None],
    )
    (
        fc_out_grad, fc_in_grad, qkv_grad, out_grad, block_out, tokens_grad,
        gain_grad, bias_grad, fc_in_bias_grad, fc_out_bias_grad,
    ) = call_widen(*parts)
    return (
        block_out[None],
        tokens_grad[None],
        gain_grad[0],
        bias_grad[0],
        qkv_grad.transpose(1, 0, 2),
        out_grad,
        fc_in_grad,
        fc_in_bias_grad[0],
        fc_out_grad,
        fc_out_bias_grad[0],
    )


def solution(mesh):
    placed = (
        P("seq", "ctx", None), P("seq", "ctx"), P("seq", "ctx", None), P(), P(),
        P(None, None, "tp"), P("tp", None), P(None, "tp"), P("tp"), P("tp", None), P(),
    )
    return jax.shard_map(
        local,
        mesh=mesh,
        in_specs=placed,
        out_specs=(
            P("seq", "ctx", None), P("seq", "ctx", None), P(), P(), P(None, None, "tp"),
            P("tp", None), P(None, "tp"), P("tp"), P("tp", None), P(),
        ),
        check_vma=False,
    )
```

time: 170 us -> 146 us (0.86)
  Pallas kernels: 164 us -> 145 us
  local copies, waits for them, and re-layouts: 4.61 us -> 0 us
    pallas_call x1, Pallas kernels: 150 us -> 130 us  [call_layer(): pl.pallas_call(layer_kernel, name='layer', out_shape=(jax.ShapeDtypeStruc...]
    unnamed x8 -> x0, local copies, waits for them, and re-layouts: 3.14 us -> none
where the time goes in v2:
time: 146 us
  Pallas kernels  145 us (99%)
    pallas_call x1, Pallas kernels, call_layer(): pl.pallas_call(layer_kernel, name='layer', out_shape=(jax.ShapeDtypeStruc...  130 us
    pallas_call x1, Pallas kernels, call_widen(): pl.pallas_call(widen_kernel, name='widen', grid=(n,), in_specs=[spec((1,...  15.1 us

profile of v2, /device:TPU:1, one launch (start us, length us, event | category | flops | bytes accessed | tf_op | source)
XLA Modules:
  0.0 146.0 jit_solution(3071411569345874780)
XLA Ops:
  0.6 130.1 %layer.1 = (bf16[256,1024]{1,0:T(8,128)(2,1)}, f32[256,1024]{1,0:T(8,128)}, f32[8,1024]{1,0:T(8,128)}, bf16[2,2,1024,512]{3,2,1,0:T(8,128)(2,1)}, bf16[2,2,1024,...) custom-call(s32[1,256]{1,0:T(1,128)} %pos_h.1, ...), custom_call_target="tpu_custom_call" | custom-call | tf_op jit(solution)/shard_map/layer/pallas_call | solution.py:631
  130.8 15.1 %widen.1 = (f32[2048,1024]{1,0:T(8,128)}, f32[1024,2048]{1,0:T(8,128)}, f32[3,1024,512]{2,1,0:T(8,128)}, f32[512,1024]{1,0:T(8,128)}, bf16[256,1024]{1,0:T(8,128...) custom-call(bf16[2,2,1024,512]{3,2,1,0:T(8,128)(2,1)} %get-tuple-ele, ...), custom_call_target="tpu_custom_call" | custom-call | tf_op jit(solution)/shard_map/widen/pallas_call | solution.py:698

commit v3 on v2

--- a/solution.py
+++ b/solution.py
@@ -21,6 +21,7 @@
 ROWS = (1024, 1024, 1024, 512)
 WIDE = (512, 512, 384, 256)
 ORDER = ("xz", "xz", "xz", "xz")
+Y_FIRST = (True, True, False, False)
 
 
 def dot(a, b):
@@ -60,19 +61,15 @@
         u, v = (1 - c) * x + c * z, (1 - c) * z + c * x
         one, three = pick(me.x_one, me.z_one), pick(me.x_three, me.z_three)
         self.before, self.after = (one, three), (three, one)
-        u0, u1 = u % 2, u // 2
-        w0 = 1 - u0
-        self.keep = (2 * xor(u0, u1) + u1, 2 * u1 + u0)
-        self.give = (2 * xor(u0, u1) + 1 - u1, 2 * u1 + 1 - u0)
-        self.their_give = (2 * xor(w0, u1) + 1 - u1, 2 * (1 - u1) + u0)
-        self.their_keep = (2 * xor(w0, u1) + u1, 2 * (1 - u1) + 1 - u0)
-        self.place = v * 2 + me.yh
+        flip = u + 1 - 2 * (u % 2)
+        self.keep, self.give = (u, u), (3 - u, flip)
+        self.their_give, self.their_keep = (lax.rem(u + 2, 4),) * 2, (flip, 3 - u)
+        self.v = v
         self.others = []
-        for k in range(1, 8):
-            to = lax.rem(self.place + k, 8)
-            there = to // 2
-            zz, xx = (1 - c) * there + c * z, (1 - c) * x + c * there
-            self.others.append((to, (zz * 2 + me.core, xx * 2 + to % 2, me.tp)))
+        for k in range(1, 4):
+            to = lax.rem(v + k, 4)
+            zz, xx = (1 - c) * to + c * z, (1 - c) * x + c * to
+            self.others.append((to, (zz * 2 + me.core, xx * 2 + me.yh, me.tp)))
 
 
 def remote(src, dst, send, recv, device):
@@ -98,14 +95,14 @@
     out_b, out_t, out_s, out_0, out_1, out_2, out_3,
     pos, tok, cot, nrm, xhat, inv, wqkv, wout, fin, fout, tabs, send1, land1, ptile, pland, psm, qg, kv,
     kvt, sbuf, pbuf, atts, aq, send2, land2, sib_att, send3, land3, act_o, act_b, gh_o, gh_b, lf_o, lf_b,
-    nrm_t, tps, tpl, g0, g1, g2, g3, l0, l1, l2, l3, r0, r1, r2, r3, t0, t1, t2, t3, w0, w1, w2, w3, vs,
-    vw, blk, tgr, in_sem, sib_s, sib_r, all_s, all_r, tp_s, tp_r, rs_s, rs_r, fw_s, fw_r, st_s, v_s, v_r,
-    o_s,
+    nrm_t, tps, tpl, g0, g1, g2, g3, l0, l1, l2, l3, r0, r1, r2, r3, t0, t1, t2, t3, y0, y1, y2, y3, w0,
+    w1, w2, w3, vs, vw, blk, tgr, in_sem, sib_s, sib_r, all_s, all_r, tp_s, tp_r, rs_s, rs_r, fw_s, fw_r,
+    st_s, v_s, v_r, o_s,
 ):
     me = Place()
     core, ctx = me.core, me.ctx
     g, lands, res, outs = (g0, g1, g2, g3), (l0, l1, l2, l3), (r0, r1, r2, r3), (out_0, out_1, out_2, out_3)
-    slots, whole_q = (t0, t1, t2, t3), (w0, w1, w2, w3)
+    slots, ybuf, whole_q = (t0, t1, t2, t3), (y0, y1, y2, y3), (w0, w1, w2, w3)
 
     loads = [
         pltpu.make_async_copy(a, b, in_sem.at[i])
@@ -121,11 +118,24 @@
 
     barrier = pltpu.get_barrier_semaphore()
     peers = [(me.seq, lax.rem(ctx + k, 8), me.tp) for k in range(1, 8)]
-    across = [
-        ((lax.rem(me.z + k, 4) * 2 + core, me.x * 2 + yh, me.tp)) for k in range(1, 4) for yh in range(2)
-    ]
+    across = [(lax.rem(me.z + k, 4) * 2 + core, ctx, me.tp) for k in range(1, 4)]
     for device in peers + across + [me.sib, me.other_tp]:
         pl.semaphore_signal(barrier, inc=1, device_id=device, device_id_type=MESH)
+
+    loads[1].wait()
+
+    def norm_rows(i, _):
+        rows = pl.ds(pl.multiple_of(i * 64, 64), 64)
+        x = tok[rows, :].astype(F32)
+        x = x - jnp.mean(x, axis=-1, keepdims=True)
+        inv_std = lax.rsqrt(jnp.mean(x * x, axis=-1, keepdims=True) + EPS)
+        x = x * inv_std
+        xhat[rows, :] = x
+        inv[rows, :] = jnp.broadcast_to(inv_std, (64, 128))
+        nrm[0, rows, :] = (x * gain[...] + lnb[...]).astype(BF)
+        return 0
+
+    lax.fori_loop(0, T // 64, norm_rows, 0)
 
     loads[0].wait()
     first = pos[0, 0]
@@ -142,23 +152,8 @@
     tabs[2] = jnp.where(lane % 2 == 0, 0.0, sine)
     ptile[...] = jnp.full((8, 128), first, jnp.int32)
 
-    loads[1].wait()
-
-    def norm_rows(i, _):
-        rows = pl.ds(pl.multiple_of(i * 64, 64), 64)
-        x = tok[rows, :].astype(F32)
-        x = x - jnp.mean(x, axis=-1, keepdims=True)
-        inv_std = lax.rsqrt(jnp.mean(x * x, axis=-1, keepdims=True) + EPS)
-        x = x * inv_std
-        xhat[rows, :] = x
-        inv[rows, :] = jnp.broadcast_to(inv_std, (64, 128))
-        nrm[0, rows, :] = (x * gain[...] + lnb[...]).astype(BF)
-        return 0
-
-    lax.fori_loop(0, T // 64, norm_rows, 0)
-
     loads[2].wait()
-    pl.semaphore_wait(barrier, 15)
+    pl.semaphore_wait(barrier, 12)
 
     sib_pairs = (
         (cot.at[0], cot.at[1]),
@@ -201,7 +196,13 @@
         send1[2 * e, :, 128:256] = jnp.where(low_lane, k, swap(v)).astype(BF)
         send1[2 * e + 1, :, 0:128] = jnp.where(low_lane, swap(q), ga).astype(BF)
         send1[2 * e + 1, :, 128:256] = jnp.where(low_lane, swap(k), v).astype(BF)
-    to_all(send1, land1, 1)
+        for d in (2 * e, 2 * e + 1):
+
+            @pl.when(ctx != d)
+            def _():
+                remote(send1.at[d], land1.at[ctx], all_s.at[1], all_r.at[1], (me.seq, d, me.tp)).start()
+
+    land1[ctx] = send1[ctx]
 
     loads[5].wait()
     loads[6].wait()
@@ -278,63 +279,99 @@
             add(m, h, None, ROWS[m] // 4, me.order[m].give[h] * (ROWS[m] // 4), 0)
             swap_copy(m, h, 2).start()
 
+    def rows_of(m, v, y, wide):
+        n = ROWS[m] // 32
+        start = (y * 4 + v) * n if Y_FIRST[m] else (v * 2 + y) * n
+        return pl.ds(pl.multiple_of(start, 16), n * wide)
+
+    def along_v(m, ref, i, slot):
+        o = me.order[m]
+        for to, device in o.others:
+            if slot:
+                src = ref.at[:, rows_of(m, to, me.yh, 1) if Y_FIRST[m] else rows_of(m, to, 0, 2)]
+                dst = slots[m].at[o.v]
+            else:
+                src = ref.at[:, rows_of(m, o.v, me.yh, 1) if Y_FIRST[m] else rows_of(m, o.v, 0, 2)]
+                dst = src
+            remote(src, dst, rs_s.at[m, i - 1], rs_r.at[m, i], device).start()
+
+    def along_y(m, ref, i, slot):
+        o = me.order[m]
+        y = 1 - me.yh if slot else me.yh
+        src = ref.at[:, rows_of(m, 0, y, 4) if Y_FIRST[m] else rows_of(m, o.v, y, 1)]
+        remote(src, ybuf[m] if slot else src, rs_s.at[m, i - 1], rs_r.at[m, i], me.y).start()
+
+    def sum_v(m, into):
+        o = me.order[m]
+        here = rows_of(m, o.v, me.yh, 1) if Y_FIRST[m] else rows_of(m, o.v, 0, 2)
+        slots[m][o.v] = lands[m][2, :, here, :]
+        for h in range(2):
+            total = slots[m][0, h].astype(F32)
+            for k in range(1, 4):
+                total = total + slots[m][k, h].astype(F32)
+            into[h, here, :] = total.astype(BF)
+
+    def sum_y(m, into):
+        here = rows_of(m, 0, me.yh, 4) if Y_FIRST[m] else rows_of(m, me.order[m].v, me.yh, 1)
+        for h in range(2):
+            total = lands[m][2, h, here, :].astype(F32) + ybuf[m][h].astype(F32)
+            into[h, here, :] = total.astype(BF)
+
+    def three(m):
+        return slots[m].at[pl.ds(0, 3)]
+
     def second_sum(m):
         arrived(m, lands[m].at[pl.ds(1, 2)], 1)
         for h in range(2):
             add(m, h, 2, ROWS[m] // 4, me.order[m].keep[h] * (ROWS[m] // 4), 1, 2)
-        o, n = me.order[m], ROWS[m] // 32
-        for to, device in o.others:
-            piece = lands[m].at[2, :, pl.ds(pl.multiple_of(to * n, n), n)]
-            remote(piece, slots[m].at[o.place], rs_s.at[m, 1], rs_r.at[m, 2], device).start()
+        (along_y if Y_FIRST[m] else along_v)(m, lands[m].at[2], 2, True)
 
     def third_sum(m):
-        seven = slots[m].at[pl.ds(0, 7)]
-        arrived(m, seven, 2)
-        o, n = me.order[m], ROWS[m] // 32
-        here = pl.ds(pl.multiple_of(o.place * n, n), n)
-        slots[m][o.place] = lands[m][2, :, here, :]
-        for h in range(2):
-            total = slots[m][0, h].astype(F32)
-            for k in range(1, 8):
-                total = total + slots[m][k, h].astype(F32)
-            whole_q[m][h, here, :] = total.astype(BF)
-        piece = whole_q[m].at[:, here]
-        for to, device in o.others:
-            remote(piece, piece, rs_s.at[m, 2], rs_r.at[m, 3], device).start()
+        arrived(m, ybuf[m] if Y_FIRST[m] else three(m), 2)
+        (sum_y if Y_FIRST[m] else sum_v)(m, lands[m].at[2])
+        (along_v if Y_FIRST[m] else along_y)(m, lands[m].at[2], 3, True)
+
+    def fourth_sum(m):
+        arrived(m, three(m) if Y_FIRST[m] else ybuf[m], 3)
+        (sum_v if Y_FIRST[m] else sum_y)(m, whole_q[m])
+        (along_v if Y_FIRST[m] else along_y)(m, whole_q[m], 4, False)
+
+    def zeroth_gather(m):
+        arrived(m, three(m) if Y_FIRST[m] else ybuf[m], 4)
+        (along_y if Y_FIRST[m] else along_v)(m, whole_q[m], 5, False)
 
     def hand_over(m, h, src, q):
         there = outs[m].at[core, h, quarter(m, q)]
         remote(src, there, fw_s.at[m], fw_r.at[m], me.sib).start()
         pltpu.make_async_copy(src, there, st_s.at[m]).start()
 
-    def spread(m, h, src, q, k):
+    def spread(m, h, src, k):
         o = me.order[m]
         device = (o.before if k else o.after)[h]
-        remote(src, res[m].at[h, quarter(m, q)], rs_s.at[m, 3], rs_r.at[m, 4 + k], device).start()
+        remote(src, res[m].at[k, h], rs_s.at[m, 5], rs_r.at[m, 6 + min(k, 1)], device).start()
 
     def first_gather(m):
-        arrived(m, slots[m].at[pl.ds(0, 7)], 3)
+        arrived(m, ybuf[m] if Y_FIRST[m] else three(m), 5)
         o = me.order[m]
         for k in range(2):
             for h in range(2):
-                spread(m, h, whole_q[m].at[h], o.keep[h], k)
+                spread(m, h, whole_q[m].at[h], k)
         for h in range(2):
             hand_over(m, h, whole_q[m].at[h], o.keep[h])
 
     def second_gather(m):
-        arrived(m, lands[m].at[0], 4)
+        arrived(m, lands[m].at[0], 6)
         o = me.order[m]
         for h in range(2):
-            src = res[m].at[h, quarter(m, o.give[h])]
-            spread(m, h, src, o.give[h], 1)
-            hand_over(m, h, src, o.give[h])
+            spread(m, h, res[m].at[0, h], 2)
+            hand_over(m, h, res[m].at[0, h], o.give[h])
 
     def third_gather(m):
-        arrived(m, lands[m].at[pl.ds(0, 2)], 5)
+        arrived(m, lands[m].at[pl.ds(0, 2)], 7)
         o = me.order[m]
         for h in range(2):
-            for q in (o.their_give[h], o.their_keep[h]):
-                hand_over(m, h, res[m].at[h, quarter(m, q)], q)
+            hand_over(m, h, res[m].at[1, h], o.their_keep[h])
+            hand_over(m, h, res[m].at[2, h], o.their_give[h])
 
     def outer(m, left_t, right):
         o = me.order[m]
@@ -428,71 +465,18 @@
         aq[r, 256:320, :] = dq[:, 0:128]
         aq[r, 320:384, :] = dq[:, 128:256]
 
-    ahead = scores(7)
-    for r in range(7, -1, -1):
-        now = ahead
-        if r:
-            ahead = scores(r - 1)
-        weigh(r, now)
-    for c in range(8):
-        send2[c] = atts[rank[c]]
-    to_all(send2, land2, 2)
-    back(7)
-    back(6)
-    back(5)
-    first_sum(0)
-    back(4)
-    back(3)
-    first_sum(1)
-    back(2)
-    back(1)
-    back(0)
-    for c in range(8):
-        send3[c] = aq[rank[c]]
-    to_all(send3, land3, 3)
-
     own, oth = pl.multiple_of(core * 1024, 1024), pl.multiple_of((1 - core) * 1024, 1024)
-    all_seven(land2, 2).wait_recv()
-    to_sib(4).start()
-    att_rows = land2[...].reshape(L, T).T
-
-    def branch(i, _):
-        cols = pl.ds(pl.multiple_of(i * 256, 256), 256)
-        part = dot(act_b[0], fout[pl.ds(own, 1024), cols]) + dot(act_o[...], fout[pl.ds(oth, 1024), cols])
-        tps[0, i] = (part + dot(att_rows, wout[:, cols])).astype(BF)
-        return 0
-
-    lax.fori_loop(0, 4, branch, 0)
 
     def tp_copy(i, j):
         return remote(tps.at[i, j], tpl.at[i, j], tp_s.at[i], tp_r.at[i], me.other_tp)
 
-    def tp_start(*which):
-        for i, j in which:
-            tp_copy(i, j).start()
-
-    tp_start((0, 0), (0, 1), (0, 2), (0, 3))
-    to_sib(4).wait_recv()
-    mine = land2[pl.ds(4 * core, 4)].reshape(T, T)
-    theirs = sib_att[...].reshape(T, T)
-    for h in range(2):
-        for q in range(2):
-            cols = slice(512 * h + 256 * q, 512 * h + 256 * q + 256)
-            g3[h, 256 * q : 256 * q + 256, :] = (dot(mine, cot[0, :, cols]) + dot(theirs, cot[1, :, cols])).astype(BF)
-    for k in range(2):
-        for h in range(2):
-            swap_copy(3, h, k).start()
+    def tp_all(i):
+        return remote(tps.at[i], tpl.at[i], tp_s.at[i], tp_r.at[i], me.other_tp)
 
     def mixed(i, _):
         cols = pl.ds(pl.multiple_of(i * 256, 256), 256)
         sbuf[1, cols, :] = dot_nt(gh_b[0], fin[cols, pl.ds(own, 1024)]) + dot_nt(gh_o[...], fin[cols, pl.ds(oth, 1024)])
         return 0
-
-    lax.fori_loop(0, 4, mixed, 0)
-    second_sum(0)
-    second_sum(1)
-    third_sum(0)
-    all_seven(land3, 3).wait_recv()
 
     def gather_heads(half, ref):
         for e in range(2):
@@ -512,13 +496,6 @@
             for j, part in enumerate((dq, dk, dv)):
                 ref[:, 256 * j + 128 * e : 256 * j + 128 * e + 128] = part.astype(BF)
 
-    gather_heads(1 - core, lf_o)
-    to_sib(5).start()
-    gather_heads(core, lf_b.at[0])
-    third_sum(1)
-    to_sib(5).wait_recv()
-    outer(2, nrm_t, lf_b)
-
     def late(i, _):
         cols = pl.ds(pl.multiple_of(i * 256, 256), 256)
         grad = sbuf[1, cols, :]
@@ -531,8 +508,6 @@
         vs[0, 1:2, cols] = jnp.sum(grad, axis=0, keepdims=True)
         return 0
 
-    lax.fori_loop(0, 4, late, 0)
-
     v_to = (me.sib, me.y, me.x_one, me.x_three, me.z_one, me.z_three, me.other_tp)
 
     def v_copy(i):
@@ -548,8 +523,6 @@
             vs[i + 1] = total
             v_copy(i + 1).start()
 
-    v_copy(0).start()
-
     def finish(i, _):
         rows = pl.ds(pl.multiple_of(i * 32, 32), 32)
 
@@ -569,48 +542,114 @@
 
     to_out = [pltpu.make_async_copy(blk, out_b, o_s.at[0]), pltpu.make_async_copy(tgr, out_t, o_s.at[1])]
 
-    def tp_all(i):
-        return remote(tps.at[i], tpl.at[i], tp_s.at[i], tp_r.at[i], me.other_tp)
-
+    def branch(i, _):
+        cols = pl.ds(pl.multiple_of(i * 256, 256), 256)
+        part = dot(act_b[0], fout[pl.ds(own, 1024), cols]) + dot(act_o[...], fout[pl.ds(oth, 1024), cols])
+        tps[0, i] = (part + dot(lf_o[:, 0:L], wout[:, cols])).astype(BF)
+        return 0
+
+    first_sum(1)
+    ahead = scores(7)
+    for r in range(7, -1, -1):
+        now = ahead
+        if r:
+            ahead = scores(r - 1)
+        weigh(r, now)
+    for c in range(8):
+        send2[c] = atts[rank[c]]
+    to_all(send2, land2, 2)
+    back(7)
+    back(6)
+    first_sum(0)
+    second_sum(1)
+    back(5)
+    back(4)
+    lax.fori_loop(0, 4, mixed, 0)
+    back(3)
+    back(2)
+    back(1)
+    back(0)
+    for c in range(8):
+        send3[c] = aq[rank[c]]
+    to_all(send3, land3, 3)
+    all_seven(land2, 2).wait_recv()
+    to_sib(4).start()
+    lf_o[:, 0:L] = land2[...].reshape(L, T).T
+    lax.fori_loop(0, 4, branch, 0)
+    third_sum(1)
+    to_sib(4).wait_recv()
+    mine = land2[pl.ds(4 * core, 4)].reshape(T, T)
+    theirs = sib_att[...].reshape(T, T)
+    for h in range(2):
+        for q in range(2):
+            cols = slice(512 * h + 256 * q, 512 * h + 256 * q + 256)
+            g3[h, 256 * q : 256 * q + 256, :] = (dot(mine, cot[0, :, cols]) + dot(theirs, cot[1, :, cols])).astype(BF)
+    for k in range(2):
+        for h in range(2):
+            swap_copy(3, h, k).start()
+    second_sum(0)
+    fourth_sum(1)
+    first_sum(3)
+    tp_copy(0, 2).start()
+    all_seven(land3, 3).wait_recv()
+    gather_heads(1 - core, lf_o)
+    to_sib(5).start()
+    gather_heads(core, lf_b.at[0])
+    to_sib(5).wait_recv()
+    outer(2, nrm_t, lf_b)
+    zeroth_gather(1)
+    third_sum(0)
+    lax.fori_loop(0, 4, late, 0)
+    v_copy(0).start()
     first_sum(2)
-    tp_start((1, 0), (1, 1))
-    first_sum(3)
+    v_step(0)
+    tp_copy(1, 0).start()
+    fourth_sum(0)
+    tp_copy(0, 0).start()
+    second_sum(3)
+    v_step(1)
+    second_sum(2)
+    first_gather(1)
+    zeroth_gather(0)
+    v_step(2)
+    second_gather(1)
+    third_sum(2)
+    v_step(3)
     first_gather(0)
-    first_gather(1)
-    second_sum(2)
-    v_step(0)
-    v_step(1)
-    second_sum(3)
-    third_sum(2)
     third_sum(3)
+    fourth_sum(2)
+    fourth_sum(3)
+    tp_copy(0, 1).start()
+    tp_copy(1, 1).start()
+    zeroth_gather(2)
+    zeroth_gather(3)
+    tp_copy(1, 3).start()
+    v_step(4)
+    third_gather(1)
+    second_gather(0)
     first_gather(2)
-    v_step(2)
-    v_step(3)
+    tp_copy(0, 3).start()
+    tp_copy(1, 2).start()
+    v_step(5)
     first_gather(3)
-    second_gather(0)
-    second_gather(1)
-    tp_start((1, 2), (1, 3))
-    v_step(4)
+    third_gather(0)
     second_gather(2)
     second_gather(3)
-    v_step(5)
-    third_gather(0)
-    third_gather(1)
-    v_step(6)
+    third_gather(2)
+    third_gather(3)
     tp_all(0).wait_recv()
     tp_all(1).wait_recv()
     lax.fori_loop(0, T // 32, finish, 0)
     to_out[0].start()
     to_out[1].start()
-    third_gather(3)
-    third_gather(2)
+    v_step(6)
     for m in range(4):
-        seven = slots[m].at[pl.ds(0, 7)]
-        for i, ref in enumerate((lands[m], seven, seven, lands[m])):
+        one, other = (ybuf[m], three(m)) if Y_FIRST[m] else (three(m), ybuf[m])
+        for i, ref in enumerate((lands[m], one, other, other, one, lands[m])):
             remote(ref, ref, rs_s.at[m, i], rs_r.at[m, 0], me.sib).wait_send()
         half_out = outs[m].at[1 - core]
-        remote(res[m], half_out, fw_s.at[m], fw_r.at[m], me.sib).wait()
-        pltpu.make_async_copy(res[m], outs[m].at[core], st_s.at[m]).wait()
+        remote(g[m], half_out, fw_s.at[m], fw_r.at[m], me.sib).wait()
+        pltpu.make_async_copy(g[m], outs[m].at[core], st_s.at[m]).wait()
     for i in range(6):
         to_sib(i).wait_send()
     all_seven(pland, 0).wait_send()
@@ -649,12 +688,13 @@
             V((2, T, 1024), BF), V((T, 1024), BF), V((2, T, 1024), BF), V((T, 768), BF), V((2, T, 768), BF),
             V((2, D, T), BF), V((2, 4, T, T), BF), V((2, 4, T, T), BF), V((2, 1024, 512), BF),
             V((2, 1024, 512), BF), V((2, 1024, 384), BF), V((2, 512, 256), BF), V((3, 2, 256, 512), BF),
-            V((3, 2, 256, 512), BF), V((3, 2, 256, 384), BF), V((3, 2, 128, 256), BF), V((2, 1024, 512), BF),
-            V((2, 1024, 512), BF), V((2, 1024, 384), BF), V((2, 512, 256), BF), V((8, 2, 32, 512), BF),
-            V((8, 2, 32, 512), BF), V((8, 2, 32, 384), BF), V((8, 2, 16, 256), BF), V((2, 256, 512), BF),
+            V((3, 2, 256, 512), BF), V((3, 2, 256, 384), BF), V((3, 2, 128, 256), BF), V((3, 2, 256, 512), BF),
+            V((3, 2, 256, 512), BF), V((3, 2, 256, 384), BF), V((3, 2, 128, 256), BF), V((4, 2, 32, 512), BF),
+            V((4, 2, 32, 512), BF), V((4, 2, 64, 384), BF), V((4, 2, 32, 256), BF), V((2, 128, 512), BF),
+            V((2, 128, 512), BF), V((2, 32, 384), BF), V((2, 16, 256), BF), V((2, 256, 512), BF),
             V((2, 256, 512), BF), V((2, 256, 384), BF), V((2, 128, 256), BF), V((7, 8, D), F32), V((7, 8, D), F32),
-            V((T, D), BF), V((T, D), F32), dma(7), dma(6), dma(6), dma(4), dma(4), dma(2), dma(2), dma(4, 4),
-            dma(4, 6), dma(4), dma(4), dma(4), dma(1), dma(7), dma(3),
+            V((T, D), BF), V((T, D), F32), dma(7), dma(6), dma(6), dma(4), dma(4), dma(2), dma(2), dma(4, 6),
+            dma(4, 8), dma(4), dma(4), dma(4), dma(1), dma(7), dma(3),
         ],
         compiler_params=pltpu.CompilerParams(
             collective_id=0, has_side_effects=True, vmem_limit_bytes=63 * 2**20
@@ -665,66 +705,98 @@
 def widen_kernel(
     a, b, c, d, block, grads, small,
     fc_out, fc_in, qkv, out, block_out, tokens_grad, gain, bias, fc_in_bias, fc_out_bias,
+    va, vb, vc, vd, wa, wb, wc, wd, vblk, vtgr, read, write,
 ):
-    for half in range(2):
-        fc_out[:, 512 * half : 512 * half + 512] = a[0, half].astype(F32)
-    for core in range(2):
-        for half in range(2):
-            start = 1024 * core + 512 * half
-            fc_in[:, start : start + 512] = b[core, half].astype(F32)
-        here = 256 * core
-        qkv[0, :, here : here + 256] = c[core, 0, :, 0:256].astype(F32)
-        qkv[1, :, here : here + 128] = c[core, 0, :, 256:384].astype(F32)
-        qkv[1, :, here + 128 : here + 256] = c[core, 1, :, 0:128].astype(F32)
-        qkv[2, :, here : here + 256] = c[core, 1, :, 128:384].astype(F32)
-    for half in range(2):
-        for part in range(2):
-            start = 512 * half + 256 * part
-            out[:, start : start + 256] = d[0, half, part].astype(F32)
-    block_out[...] = block[...]
-    tokens_grad[...] = grads[...]
+    def reads(i):
+        core, part = i // 4, i % 4
+        rows = lambda n, k: pl.ds(pl.multiple_of(k * n, n), n)
+        return (
+            pltpu.make_async_copy(a.at[core, :, rows(256, part)], va.at[core, :, rows(256, part)], read.at[0, i]),
+            pltpu.make_async_copy(b.at[:, :, rows(128, i)], vb.at[:, :, rows(128, i)], read.at[1, i]),
+            pltpu.make_async_copy(c.at[:, :, rows(128, i)], vc.at[:, :, rows(128, i)], read.at[2, i]),
+            pltpu.make_async_copy(d.at[core, :, :, rows(64, part)], vd.at[core, :, :, rows(64, part)], read.at[3, i]),
+        )
+
+    def issue(i, _):
+        for copy in reads(i):
+            copy.start()
+        return 0
+
+    lax.fori_loop(0, 8, issue, 0)
+    two = [pltpu.make_async_copy(block, vblk, write.at[6]), pltpu.make_async_copy(grads, vtgr, write.at[7])]
+    for copy in two:
+        copy.start()
     gain[...] = small[0:1, :]
     bias[...] = small[1:2, :]
     fc_in_bias[:, 0:1024] = small[2:3, :]
     fc_in_bias[:, 1024:2048] = small[3:4, :]
     fc_out_bias[...] = small[4:5, :]
 
+    def step(i, _):
+        core, part = i // 4, i % 4
+        copies = reads(i)
+        copies[0].wait()
+        here, there = pl.ds(pl.multiple_of(i * 256, 256), 256), pl.ds(pl.multiple_of(part * 256, 256), 256)
+        for half in range(2):
+            wa[here, 512 * half : 512 * half + 512] = va[core, half, there, :].astype(F32)
+        pltpu.make_async_copy(wa.at[here], fc_out.at[here], write.at[0]).start()
+        copies[1].wait()
+        here = pl.ds(pl.multiple_of(i * 128, 128), 128)
+        for k in range(2):
+            for half in range(2):
+                start = 1024 * k + 512 * half
+                wb[here, start : start + 512] = vb[k, half, here, :].astype(F32)
+        pltpu.make_async_copy(wb.at[here], fc_in.at[here], write.at[1]).start()
+        copies[2].wait()
+        for k in range(2):
+            at = 256 * k
+            wc[0, here, at : at + 256] = vc[k, 0, here, 0:256].astype(F32)
+            wc[1, here, at : at + 128] = vc[k, 0, here, 256:384].astype(F32)
+            wc[1, here, at + 128 : at + 256] = vc[k, 1, here, 0:128].astype(F32)
+            wc[2, here, at : at + 256] = vc[k, 1, here, 128:384].astype(F32)
+        pltpu.make_async_copy(wc.at[:, here], qkv.at[:, here], write.at[2]).start()
+        copies[3].wait()
+        here, there = pl.ds(pl.multiple_of(i * 64, 64), 64), pl.ds(pl.multiple_of(part * 64, 64), 64)
+        for half in range(2):
+            for k in range(2):
+                start = 512 * half + 256 * k
+                wd[here, start : start + 256] = vd[core, half, k, there, :].astype(F32)
+        pltpu.make_async_copy(wd.at[here], out.at[here], write.at[3]).start()
+        return 0
+
+    lax.fori_loop(0, 8, step, 0)
+    whole = [
+        pltpu.make_async_copy(src, dst, write.at[i])
+        for i, (src, dst) in enumerate(
+            ((wa, fc_out), (wb, fc_in), (wc, qkv), (wd, out), (vblk, block_out), (vtgr, tokens_grad))
+        )
+    ]
+    for i in range(2):
+        two[i].wait()
+        whole[4 + i].start()
+    for copy in whole:
+        copy.wait()
+
 
 def call_widen(block, grads, small, a, b, c, d):
-    n = 8
-    half = n // 2
-    spec = pl.BlockSpec
-    shape = jax.ShapeDtypeStruct
+    shape, V = jax.ShapeDtypeStruct, pltpu.VMEM
+    anyspace, vmem = pl.BlockSpec(memory_space=pl.ANY), pl.BlockSpec(memory_space=pltpu.VMEM)
     return pl.pallas_call(
         widen_kernel,
         name="widen",
-        grid=(n,),
-        in_specs=[
-            spec((1, 2, F // n, 512), lambda i: (i // half, 0, i % half, 0)),
-            spec((2, 2, D // n, 512), lambda i: (0, 0, i, 0)),
-            spec((2, 2, D // n, 384), lambda i: (0, 0, i, 0)),
-            spec((1, 2, 2, L // n, 256), lambda i: (i // half, 0, 0, i % half, 0)),
-            spec((T // n, D), lambda i: (i, 0)),
-            spec((T // n, D), lambda i: (i, 0)),
-            spec((8, D), lambda i: (0, 0)),
-        ],
-        out_specs=(
-            spec((F // n, D), lambda i: (i, 0)),
-            spec((D // n, F), lambda i: (i, 0)),
-            spec((3, D // n, L), lambda i: (0, i, 0)),
-            spec((L // n, D), lambda i: (i, 0)),
-            spec((T // n, D), lambda i: (i, 0)),
-            spec((T // n, D), lambda i: (i, 0)),
-            spec((1, D), lambda i: (0, 0)),
-            spec((1, D), lambda i: (0, 0)),
-            spec((1, F), lambda i: (0, 0)),
-            spec((1, D), lambda i: (0, 0)),
-        ),
+        in_specs=[anyspace] * 6 + [vmem],
+        out_specs=(anyspace,) * 6 + (vmem,) * 4,
         out_shape=(
             shape((F, D), F32), shape((D, F), F32), shape((3, D, L), F32), shape((L, D), F32),
             shape((T, D), BF), shape((T, D), F32),
             shape((1, D), F32), shape((1, D), F32), shape((1, F), F32), shape((1, D), F32),
         ),
+        scratch_shapes=[
+            V((2, 2, 1024, 512), BF), V((2, 2, 1024, 512), BF), V((2, 2, 1024, 384), BF), V((2, 2, 2, 256, 256), BF),
+            V((F, D), F32), V((D, F), F32), V((3, D, L), F32), V((L, D), F32),
+            V((T, D), BF), V((T, D), F32),
+            pltpu.SemaphoreType.DMA((4, 8)), pltpu.SemaphoreType.DMA((8,)),
+        ],
         compiler_params=pltpu.CompilerParams(vmem_limit_bytes=60 * 2**20),
     )(a, b, c, d.reshape(2, 2, 2, 256, 256), block, grads, small)
 

time: 146 us -> 130 us (0.89)
  Pallas kernels: 145 us -> 129 us
    pallas_call x1, Pallas kernels: 130 us -> 114 us  [call_layer(): pl.pallas_call(layer_kernel, name='layer', out_shape=(jax.ShapeDtypeStruc...]
where the time goes in v3:
time: 130 us
  Pallas kernels  129 us (99%)
    pallas_call x1, Pallas kernels, call_layer(): pl.pallas_call(layer_kernel, name='layer', out_shape=(jax.ShapeDtypeStruc...  114 us
    pallas_call x1, Pallas kernels, call_widen(): pl.pallas_call(widen_kernel, name='widen', in_specs=[anyspace] * 6 + [vme...  14.8 us

profile of v3, /device:TPU:1, one launch (start us, length us, event | category | flops | bytes accessed | tf_op | source)
XLA Modules:
  0.0 129.9 jit_solution(6176111880802797196)
XLA Ops:
  0.6 114.3 %layer.1 = (bf16[256,1024]{1,0:T(8,128)(2,1)}, f32[256,1024]{1,0:T(8,128)}, f32[8,1024]{1,0:T(8,128)}, bf16[2,2,1024,512]{3,2,1,0:T(8,128)(2,1)}, bf16[2,2,1024,...) custom-call(s32[1,256]{1,0:T(1,128)} %pos_h.1, ...), custom_call_target="tpu_custom_call" | custom-call | tf_op jit(solution)/shard_map/layer/pallas_call | solution.py:670
  114.9 14.8 %widen.1 = (f32[2048,1024]{1,0:T(8,128)}, f32[1024,2048]{1,0:T(8,128)}, f32[3,1024,512]{2,1,0:T(8,128)}, f32[512,1024]{1,0:T(8,128)}, bf16[256,1024]{1,0:T(8,128...) custom-call(bf16[2,2,1024,512]{3,2,1,0:T(8,128)(2,1)} %get-tuple-ele, ...), custom_call_target="tpu_custom_call" | custom-call | tf_op jit(solution)/shard_map/widen/pallas_call | solution.py:784

commit v4 on v3

--- a/solution.py
+++ b/solution.py
@@ -18,10 +18,10 @@
 BF = jnp.bfloat16
 F32 = jnp.float32
 EPS = 1e-05
-ROWS = (1024, 1024, 1024, 512)
-WIDE = (512, 512, 384, 256)
+ROWS = (1024, 1024, 1024, 1024)
+WIDE = (512, 512, 256, 256)
 ORDER = ("xz", "xz", "xz", "xz")
-Y_FIRST = (True, True, False, False)
+Y_FIRST = (1, 1, 8, 8)
 
 
 def dot(a, b):
@@ -65,11 +65,17 @@
         self.keep, self.give = (u, u), (3 - u, flip)
         self.their_give, self.their_keep = (lax.rem(u + 2, 4),) * 2, (flip, 3 - u)
         self.v = v
-        self.others = []
+        self.others, self.seven = [], []
         for k in range(1, 4):
             to = lax.rem(v + k, 4)
             zz, xx = (1 - c) * to + c * z, (1 - c) * x + c * to
             self.others.append((to, (zz * 2 + me.core, xx * 2 + me.yh, me.tp)))
+        self.place = v * 2 + me.yh
+        for k in range(1, 8):
+            to = lax.rem(self.place + k, 8)
+            there = to // 2
+            zz, xx = (1 - c) * there + c * z, (1 - c) * x + c * there
+            self.seven.append((to, (zz * 2 + me.core, xx * 2 + to % 2, me.tp)))
 
 
 def remote(src, dst, send, recv, device):
@@ -94,10 +100,10 @@
     pos_h, tok_h, cot_h, gain, lnb, wqkv_h, wout_h, fin_h, finb, fout_h, foutb,
     out_b, out_t, out_s, out_0, out_1, out_2, out_3,
     pos, tok, cot, nrm, xhat, inv, wqkv, wout, fin, fout, tabs, send1, land1, ptile, pland, psm, qg, kv,
-    kvt, sbuf, pbuf, atts, aq, send2, land2, sib_att, send3, land3, act_o, act_b, gh_o, gh_b, lf_o, lf_b,
-    nrm_t, tps, tpl, g0, g1, g2, g3, l0, l1, l2, l3, r0, r1, r2, r3, t0, t1, t2, t3, y0, y1, y2, y3, w0,
-    w1, w2, w3, vs, vw, blk, tgr, in_sem, sib_s, sib_r, all_s, all_r, tp_s, tp_r, rs_s, rs_r, fw_s, fw_r,
-    st_s, v_s, v_r, o_s,
+    kvt, sbuf, pbuf, dvt, atts, aq, send2, land2, sib_att, send3, land3, act_o, act_b, gh_o, gh_b, lf_o,
+    lf_b, nrm_t, tps, tpl, g0, g1, g2, g3, l0, l1, l2, l3, r0, r1, r2, r3, t0, t1, t2, t3, y0, y1, y2, y3,
+    w0, w1, w2, w3, vs, vw, blk, tgr, in_sem, sib_s, sib_r, all_s, all_r, tp_s, tp_r, rs_s, rs_r, fw_s,
+    fw_r, st_s, v_s, v_r, o_s,
 ):
     me = Place()
     core, ctx = me.core, me.ctx
@@ -118,7 +124,7 @@
 
     barrier = pltpu.get_barrier_semaphore()
     peers = [(me.seq, lax.rem(ctx + k, 8), me.tp) for k in range(1, 8)]
-    across = [(lax.rem(me.z + k, 4) * 2 + core, ctx, me.tp) for k in range(1, 4)]
+    across = [(lax.rem(me.z + k, 4) * 2 + core, me.x * 2 + yh, me.tp) for k in range(1, 4) for yh in range(2)]
     for device in peers + across + [me.sib, me.other_tp]:
         pl.semaphore_signal(barrier, inc=1, device_id=device, device_id_type=MESH)
 
@@ -153,7 +159,7 @@
     ptile[...] = jnp.full((8, 128), first, jnp.int32)
 
     loads[2].wait()
-    pl.semaphore_wait(barrier, 12)
+    pl.semaphore_wait(barrier, 15)
 
     sib_pairs = (
         (cot.at[0], cot.at[1]),
@@ -281,29 +287,29 @@
 
     def rows_of(m, v, y, wide):
         n = ROWS[m] // 32
-        start = (y * 4 + v) * n if Y_FIRST[m] else (v * 2 + y) * n
+        start = (y * 4 + v) * n if Y_FIRST[m] == 1 else (v * 2 + y) * n
         return pl.ds(pl.multiple_of(start, 16), n * wide)
 
     def along_v(m, ref, i, slot):
         o = me.order[m]
         for to, device in o.others:
             if slot:
-                src = ref.at[:, rows_of(m, to, me.yh, 1) if Y_FIRST[m] else rows_of(m, to, 0, 2)]
+                src = ref.at[:, rows_of(m, to, me.yh, 1) if Y_FIRST[m] == 1 else rows_of(m, to, 0, 2)]
                 dst = slots[m].at[o.v]
             else:
-                src = ref.at[:, rows_of(m, o.v, me.yh, 1) if Y_FIRST[m] else rows_of(m, o.v, 0, 2)]
+                src = ref.at[:, rows_of(m, o.v, me.yh, 1) if Y_FIRST[m] == 1 else rows_of(m, o.v, 0, 2)]
                 dst = src
             remote(src, dst, rs_s.at[m, i - 1], rs_r.at[m, i], device).start()
 
     def along_y(m, ref, i, slot):
         o = me.order[m]
         y = 1 - me.yh if slot else me.yh
-        src = ref.at[:, rows_of(m, 0, y, 4) if Y_FIRST[m] else rows_of(m, o.v, y, 1)]
+        src = ref.at[:, rows_of(m, 0, y, 4) if Y_FIRST[m] == 1 else rows_of(m, o.v, y, 1)]
         remote(src, ybuf[m] if slot else src, rs_s.at[m, i - 1], rs_r.at[m, i], me.y).start()
 
     def sum_v(m, into):
         o = me.order[m]
-        here = rows_of(m, o.v, me.yh, 1) if Y_FIRST[m] else rows_of(m, o.v, 0, 2)
+        here = rows_of(m, o.v, me.yh, 1) if Y_FIRST[m] == 1 else rows_of(m, o.v, 0, 2)
         slots[m][o.v] = lands[m][2, :, here, :]
         for h in range(2):
             total = slots[m][0, h].astype(F32)
@@ -312,10 +318,28 @@
             into[h, here, :] = total.astype(BF)
 
     def sum_y(m, into):
-        here = rows_of(m, 0, me.yh, 4) if Y_FIRST[m] else rows_of(m, me.order[m].v, me.yh, 1)
+        here = rows_of(m, 0, me.yh, 4) if Y_FIRST[m] == 1 else rows_of(m, me.order[m].v, me.yh, 1)
         for h in range(2):
             total = lands[m][2, h, here, :].astype(F32) + ybuf[m][h].astype(F32)
             into[h, here, :] = total.astype(BF)
+
+    def eighth(m, place):
+        n = ROWS[m] // 32
+        return pl.ds(pl.multiple_of(place * n, n), n)
+
+    def sum_seven(m):
+        arrived(m, slots[m].at[pl.ds(0, 7)], 2)
+        o = me.order[m]
+        here = eighth(m, o.place)
+        slots[m][o.place] = lands[m][2, :, here, :]
+        for h in range(2):
+            total = slots[m][0, h].astype(F32)
+            for k in range(1, 8):
+                total = total + slots[m][k, h].astype(F32)
+            whole_q[m][h, here, :] = total.astype(BF)
+        piece = whole_q[m].at[:, here]
+        for to, device in o.seven:
+            remote(piece, piece, rs_s.at[m, 2], rs_r.at[m, 5], device).start()
 
     def three(m):
         return slots[m].at[pl.ds(0, 3)]
@@ -324,21 +348,29 @@
         arrived(m, lands[m].at[pl.ds(1, 2)], 1)
         for h in range(2):
             add(m, h, 2, ROWS[m] // 4, me.order[m].keep[h] * (ROWS[m] // 4), 1, 2)
-        (along_y if Y_FIRST[m] else along_v)(m, lands[m].at[2], 2, True)
+        if Y_FIRST[m] == 8:
+            o = me.order[m]
+            for to, device in o.seven:
+                piece = lands[m].at[2, :, eighth(m, to)]
+                remote(piece, slots[m].at[o.place], rs_s.at[m, 1], rs_r.at[m, 2], device).start()
+            return
+        (along_y if Y_FIRST[m] == 1 else along_v)(m, lands[m].at[2], 2, True)
 
     def third_sum(m):
-        arrived(m, ybuf[m] if Y_FIRST[m] else three(m), 2)
-        (sum_y if Y_FIRST[m] else sum_v)(m, lands[m].at[2])
-        (along_v if Y_FIRST[m] else along_y)(m, lands[m].at[2], 3, True)
+        if Y_FIRST[m] == 8:
+            return sum_seven(m)
+        arrived(m, ybuf[m] if Y_FIRST[m] == 1 else three(m), 2)
+        (sum_y if Y_FIRST[m] == 1 else sum_v)(m, lands[m].at[2])
+        (along_v if Y_FIRST[m] == 1 else along_y)(m, lands[m].at[2], 3, True)
 
     def fourth_sum(m):
-        arrived(m, three(m) if Y_FIRST[m] else ybuf[m], 3)
-        (sum_v if Y_FIRST[m] else sum_y)(m, whole_q[m])
-        (along_v if Y_FIRST[m] else along_y)(m, whole_q[m], 4, False)
+        arrived(m, three(m) if Y_FIRST[m] == 1 else ybuf[m], 3)
+        (sum_v if Y_FIRST[m] == 1 else sum_y)(m, whole_q[m])
+        (along_v if Y_FIRST[m] == 1 else along_y)(m, whole_q[m], 4, False)
 
     def zeroth_gather(m):
-        arrived(m, three(m) if Y_FIRST[m] else ybuf[m], 4)
-        (along_y if Y_FIRST[m] else along_v)(m, whole_q[m], 5, False)
+        arrived(m, three(m) if Y_FIRST[m] == 1 else ybuf[m], 4)
+        (along_y if Y_FIRST[m] == 1 else along_v)(m, whole_q[m], 5, False)
 
     def hand_over(m, h, src, q):
         there = outs[m].at[core, h, quarter(m, q)]
@@ -351,7 +383,8 @@
         remote(src, res[m].at[k, h], rs_s.at[m, 5], rs_r.at[m, 6 + min(k, 1)], device).start()
 
     def first_gather(m):
-        arrived(m, ybuf[m] if Y_FIRST[m] else three(m), 5)
+        last = slots[m].at[pl.ds(0, 7)] if Y_FIRST[m] == 8 else ybuf[m] if Y_FIRST[m] == 1 else three(m)
+        arrived(m, last, 5)
         o = me.order[m]
         for k in range(2):
             for h in range(2):
@@ -440,30 +473,36 @@
             att = att + dot(kvt[HD:, keys(j)], low)
         scale = 1.0 / jnp.sum(total, axis=0, keepdims=True)
         att = att * scale
-        atts[r] = att.astype(BF)
+        atts[r, 0:HD, :] = att.astype(BF)
         both_lanes = qg[keys(r), :]
         ga_t = (both_lanes.T.astype(F32)[HD:, :] * scale).astype(BF)
         deltas[r] = jnp.sum(ga_t.astype(F32) * att, axis=0, keepdims=True)
         ga = jnp.concatenate([jnp.zeros((HD, T), BF), ga_t], axis=0).T
         qg[keys(r), :] = jnp.where(low_lane, both_lanes, ga)
+        for j in range(r + 1):
+            update = dot_nt(ga_t, pbuf[tri(r) + j * T : tri(r) + j * T + T, :])
+            if r == 7:
+                dvt[j] = update
+            else:
+                dvt[j] += update
+        atts[r, HD:, :] = dvt[r].astype(BF)
 
     def back(r):
-        q, ga = split(r)
+        _, ga = split(r)
+        q_t = qg[keys(r), :].T[0:HD, :]
         dq = jnp.zeros((HD, T), F32)
         for j in range(r + 1):
             prob = pbuf[tri(r) + j * T : tri(r) + j * T + T, :]
             dp = dot_nt(kv[keys(j), :], ga)
             ds = (prob.astype(F32) * (dp - deltas[r])).astype(BF)
-            update = dot(ds, q) + dot(prob, ga)
+            update = dot_nt(q_t, ds)
             if r == 7:
-                sbuf[0, keys(j), 0:128] = update
+                sbuf[0, j * HD : j * HD + HD, :] = update
             else:
-                sbuf[0, keys(j), 0:128] += update
+                sbuf[0, j * HD : j * HD + HD, :] += update
             dq = dq + dot(kvt[:HD, keys(j)], ds)
-        dq = (dq * HD ** (-0.5)).astype(BF)
-        aq[r, 0:256, :] = sbuf[0, keys(r), 0:128].astype(BF)
-        aq[r, 256:320, :] = dq[:, 0:128]
-        aq[r, 320:384, :] = dq[:, 128:256]
+        aq[r, 0:HD, :] = (dq * HD ** (-0.5)).astype(BF)
+        aq[r, HD:, :] = sbuf[0, r * HD : r * HD + HD, :].astype(BF)
 
     own, oth = pl.multiple_of(core * 1024, 1024), pl.multiple_of((1 - core) * 1024, 1024)
 
@@ -475,25 +514,18 @@
 
     def mixed(i, _):
         cols = pl.ds(pl.multiple_of(i * 256, 256), 256)
-        sbuf[1, cols, :] = dot_nt(gh_b[0], fin[cols, pl.ds(own, 1024)]) + dot_nt(gh_o[...], fin[cols, pl.ds(oth, 1024)])
+        grad = dot_nt(gh_b[0], fin[cols, pl.ds(own, 1024)]) + dot_nt(gh_o[...], fin[cols, pl.ds(oth, 1024)])
+        sbuf[1, cols, :] = grad + dot_nt(lf_b[0], wqkv[2, cols, :])
         return 0
 
     def gather_heads(half, ref):
+        turn = (tabs[0], -tabs[1], -tabs[2])
         for e in range(2):
             low, high = 4 * half + 2 * e, 4 * half + 2 * e + 1
-            t0, t1 = land3[low, 0:256, :].astype(F32), land3[high, 0:256, :].astype(F32)
-            dq_t = jnp.concatenate(
-                [
-                    jnp.concatenate([land3[i, 256:320, :], land3[i, 320:384, :]], axis=1)
-                    for i in (low, high)
-                ],
-                axis=0,
-            )
-            turn = (tabs[0], -tabs[1], -tabs[2])
-            dq = rotate(dq_t.T.astype(F32), *turn)
-            dk = rotate(jnp.where(low_lane, t0, swap(t1)), *turn)
-            dv = jnp.where(low_lane, swap(t0), t1)
-            for j, part in enumerate((dq, dk, dv)):
+            for j in range(2):
+                rows = slice(HD * j, HD * j + HD)
+                pair = jnp.concatenate([land3[low, rows, :], land3[high, rows, :]], axis=0)
+                part = rotate(pair.T.astype(F32), *turn)
                 ref[:, 256 * j + 128 * e : 256 * j + 128 * e + 128] = part.astype(BF)
 
     def late(i, _):
@@ -501,7 +533,7 @@
         grad = sbuf[1, cols, :]
         for ref, half in ((lf_b.at[0], core), (lf_o, 1 - core)):
             at = pl.multiple_of(half * 256, 256)
-            for j in range(3):
+            for j in range(2):
                 grad = grad + dot_nt(ref[:, 256 * j : 256 * j + 256], wqkv[j, cols, pl.ds(at, 256)])
         tps[1, i] = grad.astype(BF)
         vs[0, 0:1, cols] = jnp.sum(grad * xhat[:, cols], axis=0, keepdims=True)
@@ -545,10 +577,10 @@
     def branch(i, _):
         cols = pl.ds(pl.multiple_of(i * 256, 256), 256)
         part = dot(act_b[0], fout[pl.ds(own, 1024), cols]) + dot(act_o[...], fout[pl.ds(oth, 1024), cols])
-        tps[0, i] = (part + dot(lf_o[:, 0:L], wout[:, cols])).astype(BF)
+        tps[0, i] = (part + dot(lf_o[...], wout[:, cols])).astype(BF)
         return 0
 
-    first_sum(1)
+    first_sum(0)
     ahead = scores(7)
     for r in range(7, -1, -1):
         now = ahead
@@ -560,13 +592,12 @@
     to_all(send2, land2, 2)
     back(7)
     back(6)
-    first_sum(0)
-    second_sum(1)
     back(5)
     back(4)
-    lax.fori_loop(0, 4, mixed, 0)
+    first_sum(1)
     back(3)
     back(2)
+    second_sum(0)
     back(1)
     back(0)
     for c in range(8):
@@ -574,78 +605,88 @@
     to_all(send3, land3, 3)
     all_seven(land2, 2).wait_recv()
     to_sib(4).start()
-    lf_o[:, 0:L] = land2[...].reshape(L, T).T
+    lf_o[...] = land2[:, 0:HD, :].reshape(L, T).T
+    lf_b[0] = land2[:, HD:, :].reshape(L, T).T
     lax.fori_loop(0, 4, branch, 0)
-    third_sum(1)
+    second_sum(1)
     to_sib(4).wait_recv()
-    mine = land2[pl.ds(4 * core, 4)].reshape(T, T)
-    theirs = sib_att[...].reshape(T, T)
-    for h in range(2):
-        for q in range(2):
-            cols = slice(512 * h + 256 * q, 512 * h + 256 * q + 256)
-            g3[h, 256 * q : 256 * q + 256, :] = (dot(mine, cot[0, :, cols]) + dot(theirs, cot[1, :, cols])).astype(BF)
-    for k in range(2):
+    four = pl.ds(4 * core, 4)
+    o3 = me.order[3]
+    for k in range(4):
         for h in range(2):
-            swap_copy(3, h, k).start()
-    second_sum(0)
-    fourth_sum(1)
-    first_sum(3)
-    tp_copy(0, 2).start()
+            q = (o3.their_give, o3.their_keep, o3.give, o3.keep)[k][h]
+            rows = quarter(3, q)
+            if h == 0:
+                total = dot_nt(nrm_t[0, rows, :], land2[four, HD:, :].reshape(T, T))
+                total = total + dot_nt(nrm_t[1, rows, :], sib_att[:, HD:, :].reshape(T, T))
+            else:
+                total = dot(land2[four, 0:HD, :].reshape(T, T), cot[0, :, rows])
+                total = total + dot(sib_att[:, 0:HD, :].reshape(T, T), cot[1, :, rows])
+            g3[h, rows, :] = total.astype(BF)
+            if k < 2:
+                swap_copy(3, h, k).start()
+    tp_copy(0, 0).start()
+    third_sum(0)
+    lax.fori_loop(0, 4, mixed, 0)
     all_seven(land3, 3).wait_recv()
     gather_heads(1 - core, lf_o)
     to_sib(5).start()
     gather_heads(core, lf_b.at[0])
+    lax.fori_loop(0, 4, late, 0)
+    v_copy(0).start()
+    first_sum(3)
+    fourth_sum(0)
+    tp_copy(1, 3).start()
+    third_sum(1)
     to_sib(5).wait_recv()
     outer(2, nrm_t, lf_b)
+    v_step(0)
+    second_sum(3)
+    zeroth_gather(0)
+    v_step(1)
+    first_sum(2)
+    fourth_sum(1)
+    third_sum(3)
+    v_step(2)
+    first_gather(0)
+    second_sum(2)
     zeroth_gather(1)
-    third_sum(0)
-    lax.fori_loop(0, 4, late, 0)
-    v_copy(0).start()
-    first_sum(2)
-    v_step(0)
+    first_gather(3)
+    v_step(3)
+    second_gather(0)
+    third_sum(2)
+    tp_copy(1, 2).start()
+    tp_copy(0, 2).start()
+    tp_copy(0, 1).start()
+    second_gather(3)
+    v_step(4)
+    first_gather(1)
+    first_gather(2)
+    v_step(5)
     tp_copy(1, 0).start()
-    fourth_sum(0)
-    tp_copy(0, 0).start()
-    second_sum(3)
-    v_step(1)
-    second_sum(2)
-    first_gather(1)
-    zeroth_gather(0)
-    v_step(2)
+    tp_copy(1, 1).start()
+    third_gather(3)
     second_gather(1)
-    third_sum(2)
-    v_step(3)
-    first_gather(0)
-    third_sum(3)
-    fourth_sum(2)
-    fourth_sum(3)
-    tp_copy(0, 1).start()
-    tp_copy(1, 1).start()
-    zeroth_gather(2)
-    zeroth_gather(3)
-    tp_copy(1, 3).start()
-    v_step(4)
+    third_gather(0)
+    tp_copy(0, 3).start()
+    second_gather(2)
+    v_step(6)
     third_gather(1)
-    second_gather(0)
-    first_gather(2)
-    tp_copy(0, 3).start()
-    tp_copy(1, 2).start()
-    v_step(5)
-    first_gather(3)
-    third_gather(0)
-    second_gather(2)
-    second_gather(3)
     third_gather(2)
-    third_gather(3)
     tp_all(0).wait_recv()
     tp_all(1).wait_recv()
     lax.fori_loop(0, T // 32, finish, 0)
     to_out[0].start()
     to_out[1].start()
-    v_step(6)
     for m in range(4):
-        one, other = (ybuf[m], three(m)) if Y_FIRST[m] else (three(m), ybuf[m])
-        for i, ref in enumerate((lands[m], one, other, other, one, lands[m])):
+        one, other = (ybuf[m], three(m)) if Y_FIRST[m] == 1 else (three(m), ybuf[m])
+        every = (lands[m], one, other, other, one, lands[m])
+        if Y_FIRST[m] == 8:
+            seven = slots[m].at[pl.ds(0, 7)]
+            every = (lands[m], seven, seven, None, None, lands[m])
+        for i, ref in enumerate(every):
+            if ref is None:
+                continue
             remote(ref, ref, rs_s.at[m, i], rs_r.at[m, 0], me.sib).wait_send()
         half_out = outs[m].at[1 - core]
         remote(g[m], half_out, fw_s.at[m], fw_r.at[m], me.sib).wait()
@@ -683,18 +724,19 @@
             V((T, 128), F32), V((3, D, L), BF), V((L, D), BF), V((D, F), BF), V((F, D), BF), V((3, T, 128), F32),
             V((8, T, 256), BF), V((8, T, 256), BF), V((8, 128), jnp.int32), V((8, 8, 128), jnp.int32),
             pltpu.SMEM((8, 8, 128), jnp.int32), V((8 * T, 128), BF), V((8 * T, 128), BF), V((128, 8 * T), BF),
-            V((2, 8 * T, T), F32), V((36 * T, T), BF), V((8, HD, T), BF), V((8, 384, 128), BF), V((8, HD, T), BF),
-            V((8, HD, T), BF), V((4, HD, T), BF), V((8, 384, 128), BF), V((8, 384, 128), BF), V((T, 1024), BF),
-            V((2, T, 1024), BF), V((T, 1024), BF), V((2, T, 1024), BF), V((T, 768), BF), V((2, T, 768), BF),
-            V((2, D, T), BF), V((2, 4, T, T), BF), V((2, 4, T, T), BF), V((2, 1024, 512), BF),
-            V((2, 1024, 512), BF), V((2, 1024, 384), BF), V((2, 512, 256), BF), V((3, 2, 256, 512), BF),
-            V((3, 2, 256, 512), BF), V((3, 2, 256, 384), BF), V((3, 2, 128, 256), BF), V((3, 2, 256, 512), BF),
-            V((3, 2, 256, 512), BF), V((3, 2, 256, 384), BF), V((3, 2, 128, 256), BF), V((4, 2, 32, 512), BF),
-            V((4, 2, 32, 512), BF), V((4, 2, 64, 384), BF), V((4, 2, 32, 256), BF), V((2, 128, 512), BF),
-            V((2, 128, 512), BF), V((2, 32, 384), BF), V((2, 16, 256), BF), V((2, 256, 512), BF),
-            V((2, 256, 512), BF), V((2, 256, 384), BF), V((2, 128, 256), BF), V((7, 8, D), F32), V((7, 8, D), F32),
-            V((T, D), BF), V((T, D), F32), dma(7), dma(6), dma(6), dma(4), dma(4), dma(2), dma(2), dma(4, 6),
-            dma(4, 8), dma(4), dma(4), dma(4), dma(1), dma(7), dma(3),
+            V((2, 8 * T, T), F32), V((36 * T, T), BF), V((8, HD, T), F32), V((8, 2 * HD, T), BF),
+            V((8, 2 * HD, T), BF), V((8, 2 * HD, T), BF), V((8, 2 * HD, T), BF), V((4, 2 * HD, T), BF),
+            V((8, 2 * HD, T), BF), V((8, 2 * HD, T), BF), V((T, 1024), BF), V((2, T, 1024), BF), V((T, 1024), BF),
+            V((2, T, 1024), BF), V((T, L), BF), V((2, T, L), BF), V((2, D, T), BF), V((2, 4, T, T), BF),
+            V((2, 4, T, T), BF), V((2, 1024, 512), BF), V((2, 1024, 512), BF), V((2, 1024, 256), BF),
+            V((2, 1024, 256), BF), V((3, 2, 256, 512), BF), V((3, 2, 256, 512), BF), V((3, 2, 256, 256), BF),
+            V((3, 2, 256, 256), BF), V((3, 2, 256, 512), BF), V((3, 2, 256, 512), BF), V((3, 2, 256, 256), BF),
+            V((3, 2, 256, 256), BF), V((4, 2, 32, 512), BF), V((4, 2, 32, 512), BF), V((8, 2, 32, 256), BF),
+            V((8, 2, 32, 256), BF), V((2, 128, 512), BF), V((2, 128, 512), BF), V((2, 16, 256), BF),
+            V((2, 16, 256), BF), V((2, 256, 512), BF), V((2, 256, 512), BF), V((2, 256, 256), BF),
+            V((2, 256, 256), BF), V((7, 8, D), F32), V((7, 8, D), F32), V((T, D), BF), V((T, D), F32), dma(7),
+            dma(6), dma(6), dma(4), dma(4), dma(2), dma(2), dma(4, 6), dma(4, 8), dma(4), dma(4), dma(4), dma(1),
+            dma(7), dma(3),
         ],
         compiler_params=pltpu.CompilerParams(
             collective_id=0, has_side_effects=True, vmem_limit_bytes=63 * 2**20
@@ -714,7 +756,8 @@
             pltpu.make_async_copy(a.at[core, :, rows(256, part)], va.at[core, :, rows(256, part)], read.at[0, i]),
             pltpu.make_async_copy(b.at[:, :, rows(128, i)], vb.at[:, :, rows(128, i)], read.at[1, i]),
             pltpu.make_async_copy(c.at[:, :, rows(128, i)], vc.at[:, :, rows(128, i)], read.at[2, i]),
-            pltpu.make_async_copy(d.at[core, :, :, rows(64, part)], vd.at[core, :, :, rows(64, part)], read.at[3, i]),
+            pltpu.make_async_copy(d.at[:, 0, i // 2, rows(128, i % 2)], vd.at[:, 0, i // 2, rows(128, i % 2)], read.at[3, i]),
+            pltpu.make_async_copy(d.at[core, 1, :, rows(64, part)], vd.at[core, 1, :, rows(64, part)], read.at[4, i]),
         )
 
     def issue(i, _):
@@ -748,19 +791,18 @@
                 wb[here, start : start + 512] = vb[k, half, here, :].astype(F32)
         pltpu.make_async_copy(wb.at[here], fc_in.at[here], write.at[1]).start()
         copies[2].wait()
+        copies[3].wait()
+        there = pl.ds(pl.multiple_of(i % 2 * 128, 128), 128)
         for k in range(2):
-            at = 256 * k
-            wc[0, here, at : at + 256] = vc[k, 0, here, 0:256].astype(F32)
-            wc[1, here, at : at + 128] = vc[k, 0, here, 256:384].astype(F32)
-            wc[1, here, at + 128 : at + 256] = vc[k, 1, here, 0:128].astype(F32)
-            wc[2, here, at : at + 256] = vc[k, 1, here, 128:384].astype(F32)
+            at = slice(256 * k, 256 * k + 256)
+            wc[0, here, at] = vc[k, 0, here, :].astype(F32)
+            wc[1, here, at] = vc[k, 1, here, :].astype(F32)
+            wc[2, here, at] = vd[k, 0, i // 2, there, :].astype(F32)
         pltpu.make_async_copy(wc.at[:, here], qkv.at[:, here], write.at[2]).start()
-        copies[3].wait()
+        copies[4].wait()
         here, there = pl.ds(pl.multiple_of(i * 64, 64), 64), pl.ds(pl.multiple_of(part * 64, 64), 64)
-        for half in range(2):
-            for k in range(2):
-                start = 512 * half + 256 * k
-                wd[here, start : start + 256] = vd[core, half, k, there, :].astype(F32)
+        for k in range(4):
+            wd[here, 256 * k : 256 * k + 256] = vd[core, 1, k, there, :].astype(F32)
         pltpu.make_async_copy(wd.at[here], out.at[here], write.at[3]).start()
         return 0
 
@@ -792,13 +834,13 @@
             shape((1, D), F32), shape((1, D), F32), shape((1, F), F32), shape((1, D), F32),
         ),
         scratch_shapes=[
-            V((2, 2, 1024, 512), BF), V((2, 2, 1024, 512), BF), V((2, 2, 1024, 384), BF), V((2, 2, 2, 256, 256), BF),
+            V((2, 2, 1024, 512), BF), V((2, 2, 1024, 512), BF), V((2, 2, 1024, 256), BF), V((2, 2, 4, 256, 256), BF),
             V((F, D), F32), V((D, F), F32), V((3, D, L), F32), V((L, D), F32),
             V((T, D), BF), V((T, D), F32),
-            pltpu.SemaphoreType.DMA((4, 8)), pltpu.SemaphoreType.DMA((8,)),
+            pltpu.SemaphoreType.DMA((5, 8)), pltpu.SemaphoreType.DMA((8,)),
         ],
         compiler_params=pltpu.CompilerParams(vmem_limit_bytes=60 * 2**20),
-    )(a, b, c, d.reshape(2, 2, 2, 256, 256), block, grads, small)
+    )(a, b, c, d.reshape(2, 2, 4, 256, 256), block, grads, small)
 
 
 def local(

time: 130 us -> 128 us (0.985)
  Pallas kernels: 129 us -> 127 us
    pallas_call x1, Pallas kernels: 114 us -> 112 us  [call_layer(): pl.pallas_call(layer_kernel, name='layer', out_shape=(jax.ShapeDtypeStruc...]
where the time goes in v4:
time: 128 us
  Pallas kernels  127 us (99%)
    pallas_call x1, Pallas kernels, call_layer(): pl.pallas_call(layer_kernel, name='layer', out_shape=(jax.ShapeDtypeStruc...  112 us
    pallas_call x1, Pallas kernels, call_widen(): pl.pallas_call(widen_kernel, name='widen', in_specs=[anyspace] * 6 + [vme...  14.9 us

profile of v4, /device:TPU:1, one launch (start us, length us, event | category | flops | bytes accessed | tf_op | source)
XLA Modules:
  0.0 127.6 jit_solution(944035729495769904)
XLA Ops:
  0.6 111.8 %layer.1 = (bf16[256,1024]{1,0:T(8,128)(2,1)}, f32[256,1024]{1,0:T(8,128)}, f32[8,1024]{1,0:T(8,128)}, bf16[2,2,1024,512]{3,2,1,0:T(8,128)(2,1)}, bf16[2,2,1024,...) custom-call(s32[1,256]{1,0:T(1,128)} %pos_h.1, ...), custom_call_target="tpu_custom_call" | custom-call | tf_op jit(solution)/shard_map/layer/pallas_call | solution.py:711
  112.5 14.9 %widen.1 = (f32[2048,1024]{1,0:T(8,128)}, f32[1024,2048]{1,0:T(8,128)}, f32[3,1024,512]{2,1,0:T(8,128)}, f32[512,1024]{1,0:T(8,128)}, bf16[256,1024]{1,0:T(8,128...) custom-call(bf16[2,2,1024,512]{3,2,1,0:T(8,128)(2,1)} %get-tuple-ele, ...), custom_call_target="tpu_custom_call" | custom-call | tf_op jit(solution)/shard_map/widen/pallas_call | solution.py:826

commit v5 on v4

--- a/solution.py
+++ b/solution.py
@@ -658,26 +658,26 @@
     tp_copy(1, 2).start()
     tp_copy(0, 2).start()
     tp_copy(0, 1).start()
+    tp_copy(1, 0).start()
     second_gather(3)
+    tp_copy(1, 1).start()
+    tp_copy(0, 3).start()
     v_step(4)
     first_gather(1)
     first_gather(2)
     v_step(5)
-    tp_copy(1, 0).start()
-    tp_copy(1, 1).start()
     third_gather(3)
     second_gather(1)
     third_gather(0)
-    tp_copy(0, 3).start()
     second_gather(2)
     v_step(6)
     third_gather(1)
-    third_gather(2)
     tp_all(0).wait_recv()
     tp_all(1).wait_recv()
     lax.fori_loop(0, T // 32, finish, 0)
     to_out[0].start()
     to_out[1].start()
+    third_gather(2)
     for m in range(4):
         one, other = (ybuf[m], three(m)) if Y_FIRST[m] == 1 else (three(m), ybuf[m])
         every = (lands[m], one, other, other, one, lands[m])

time: 128 us -> 128 us (level)
  no operation moved by 1% of the time
where the time goes in v5:
time: 128 us
  Pallas kernels  127 us (99%)
    pallas_call x1, Pallas kernels, call_layer(): pl.pallas_call(layer_kernel, name='layer', out_shape=(jax.ShapeDtypeStruc...  112 us
    pallas_call x1, Pallas kernels, call_widen(): pl.pallas_call(widen_kernel, name='widen', in_specs=[anyspace] * 6 + [vme...  14.9 us

profile of v5, /device:TPU:1, one launch (start us, length us, event | category | flops | bytes accessed | tf_op | source)
XLA Modules:
  0.0 127.6 jit_solution(6402121014067215424)
XLA Ops:
  0.6 111.8 %layer.1 = (bf16[256,1024]{1,0:T(8,128)(2,1)}, f32[256,1024]{1,0:T(8,128)}, f32[8,1024]{1,0:T(8,128)}, bf16[2,2,1024,512]{3,2,1,0:T(8,128)(2,1)}, bf16[2,2,1024,...) custom-call(s32[1,256]{1,0:T(1,128)} %pos_h.1, ...), custom_call_target="tpu_custom_call" | custom-call | tf_op jit(solution)/shard_map/layer/pallas_call | solution.py:711
  112.5 14.9 %widen.1 = (f32[2048,1024]{1,0:T(8,128)}, f32[1024,2048]{1,0:T(8,128)}, f32[3,1024,512]{2,1,0:T(8,128)}, f32[512,1024]{1,0:T(8,128)}, bf16[256,1024]{1,0:T(8,128...) custom-call(bf16[2,2,1024,512]{3,2,1,0:T(8,128)(2,1)} %get-tuple-ele, ...), custom_call_target="tpu_custom_call" | custom-call | tf_op jit(solution)/shard_map/widen/pallas_call | solution.py:826
